TPU v7x, 32 devices: a whole 2x2x4 slice. The times are simulated.
32 devices in a mesh: energy: 16 (over z, y, x), mom: 2 (over core).
Axes of the slice: x: 2, y: 2, z: 4, core: 2. Of those that a mesh axis runs over, the one named last changes fastest.
Arguments:
- lesser: bfloat16 [2, 2, 512, 65536], P('mom', None, 'energy'), may hold values from -6 to 6
- greater: bfloat16 [2, 2, 512, 65536], P('mom', None, 'energy'), may hold values from -6 to 6
- coulomb: bfloat16 [2, 4, 128, 128], P('mom'), may hold values from -0.375 to 0.375
- tile_block: int32 [4], replicated, may hold values from 0 to 3, each once
- shift_table: int32 [2, 2], replicated, may hold values from 0 to 1, each once within a row
Outputs:
- polarization: bfloat16 [2, 2, 512, 65536], P('mom', None, 'energy')
- screened: float32 [2, 2, 128, 65536], P('mom', None, 'energy')
Inputs may be any that keep to these rules, and one draw needn't show every extreme that they name: `tile_block`: each of the 4 tiles holds a different block of the pattern. `shift_table`: each row names every momentum once.
All inputs are finite; a program needn't handle non-finite values.
Results may differ from a plain program's by a relative error of at most 0.0013.
Values may be sent and summed in bfloat16 or wider, within the bound.
No kernel may reach another device: no remote copies, remote signals or barrier semaphores. Data moves between devices by JAX's collectives and lax.ppermute only.
A program may use at most 256 MiB of HBM per device.

v0:
```python
import math

import jax
import jax.numpy as jnp
from jax import lax
from jax.sharding import PartitionSpec as P

E = 512


def rotation(product, period, sign):
    angle = 2.0 * math.pi / period * (product % period).astype(jnp.float32)
    return (jnp.cos(angle), sign * jnp.sin(angle))


def complex_einsum(form, table_re, table_im, data_re, data_im, data_axis):
    upper = jnp.concatenate((table_re, -table_im), axis=1)
    lower = jnp.concatenate((table_im, table_re), axis=1)
    table = jnp.concatenate((upper, lower), axis=0)
    data = jnp.concatenate((data_re, data_im), axis=data_axis)
    result = jnp.einsum(
        form, table, data, precision=lax.Precision.HIGH, preferred_element_type=jnp.float32
    )
    half = table_re.shape[0]
    return (result[:half], result[half:])


def transform(data_re, data_im, length, sign):
    radix = 32
    rows, width = data_re.shape
    outer = length // radix
    inner = rows // radix
    shaped_re = data_re.reshape(inner, radix, width)
    shaped_im = data_im.reshape(inner, radix, width)
    freq = jnp.arange(outer, dtype=jnp.int32)
    first_re, first_im = rotation(
        freq[:, None] * jnp.arange(inner, dtype=jnp.int32)[None, :], outer, sign
    )
    mid_re, mid_im = complex_einsum("kn,nmc->kmc", first_re, first_im, shaped_re, shaped_im, 0)
    twist_re, twist_im = rotation(
        freq[:, None] * jnp.arange(radix, dtype=jnp.int32)[None, :], length, sign
    )
    turned_re = mid_re * twist_re[:, :, None] - mid_im * twist_im[:, :, None]
    turned_im = mid_re * twist_im[:, :, None] + mid_im * twist_re[:, :, None]
    digits = jnp.arange(radix, dtype=jnp.int32)
    last_re, last_im = rotation(digits[:, None] * digits[None, :], radix, sign)
    out_re, out_im = complex_einsum("jm,kmc->jkc", last_re, last_im, turned_re, turned_im, 1)
    return (out_re.reshape(length, width), out_im.reshape(length, width))


def spectrum(pair, energies):
    return transform(pair[0].astype(jnp.float32), pair[1].astype(jnp.float32), 2 * energies, -1.0)


def correlate(left, right, rows, energies):
    count = left.shape[0]
    spec_left = [spectrum(left[k], energies) for k in range(count)]
    spec_right = [spectrum(right[k], energies) for k in range(count)]
    right_re = jnp.stack([item[0] for item in spec_right])
    right_im = jnp.stack([item[1] for item in spec_right])
    scale = 1.0 / (math.sqrt(count * energies) * 2 * energies)
    results = []
    for q in range(rows.shape[0]):
        total_re = jnp.zeros_like(spec_left[0][0])
        total_im = jnp.zeros_like(spec_left[0][0])
        for k in range(count):
            other_re = lax.dynamic_index_in_dim(right_re, rows[q, k], 0, keepdims=False)
            other_im = lax.dynamic_index_in_dim(right_im, rows[q, k], 0, keepdims=False)
            total_re = total_re + spec_left[k][0] * other_re + spec_left[k][1] * other_im
            total_im = total_im + spec_left[k][1] * other_re - spec_left[k][0] * other_im
        back_re, back_im = transform(total_re, total_im, 2 * energies, 1.0)
        results.append(jnp.stack([-back_im[:energies], back_re[:energies]]) * scale)
    return jnp.stack(results)


def polar_all(left, right, rows, energies):
    columns = left.shape[3]
    width = math.gcd(columns, 128)
    count_q = rows.shape[0]

    def step(index, result):
        start = index * width
        part_left = lax.dynamic_slice_in_dim(left, start, width, 3)
        part_right = lax.dynamic_slice_in_dim(right, start, width, 3)
        block = correlate(part_left, part_right, rows, energies).astype(jnp.bfloat16)
        return lax.dynamic_update_slice_in_dim(result, block, start, 3)

    empty = jnp.zeros((count_q, 2, energies, columns), jnp.bfloat16)
    return lax.fori_loop(0, columns // width, step, empty)


def reorder(back, count, groups):
    lead, parts, rows, columns = back.shape
    piece = columns // (count * groups)
    shaped = back.reshape(lead, parts, rows, count, groups, piece)
    return jnp.transpose(shaped, (0, 1, 2, 4, 3, 5)).reshape(lead, parts, rows, columns)


def screen(near, coulomb, tile_block):
    tiles_n = coulomb.shape[1]
    block = coulomb.shape[2]
    band = (tiles_n + 2) // 3
    levels = near.shape[2]
    tiles = near[0].reshape(2, levels, tiles_n, block, block)
    labels = jnp.arange(tiles_n, dtype=jnp.int32)
    onehot = tile_block[:, None] == labels[None, :]
    inverse = jnp.sum(jnp.where(onehot, labels[:, None], 0), axis=0)
    ordered = jnp.take(tiles, inverse, axis=2)
    results = []
    for r in range(band):
        for c in range(max(0, r - 1), min(band, r + 2)):
            acc = jnp.zeros((2, levels, block, block), jnp.float32)
            for l in range(max(0, r - 1), min(band, r + 2)):
                acc = acc + jnp.einsum(
                    "ij,sejk->seik",
                    coulomb[0, 2 * r + l],
                    ordered[:, :, 2 * l + c],
                    preferred_element_type=jnp.float32,
                )
            results.append(acc)
    return jnp.stack(results, axis=2).reshape(1, 2, levels, tiles_n * block * block)


def shards(lesser, greater, coulomb, tile_block, shift_table):
    count = lax.axis_size("mom")
    groups = lax.axis_size("energy")
    stacked = jnp.concatenate((lesser, greater), axis=0)
    moved = lax.all_to_all(
        lax.all_to_all(stacked, "energy", split_axis=3, concat_axis=2, tiled=True),
        "mom",
        split_axis=3,
        concat_axis=0,
        tiled=True,
    )
    moved = moved.reshape(count, 2, 2, E, moved.shape[3])
    polar_cols = polar_all(moved[:, 0], moved[:, 1], shift_table, E)
    back = lax.all_to_all(
        lax.all_to_all(polar_cols, "energy", split_axis=2, concat_axis=3, tiled=True),
        "mom",
        split_axis=0,
        concat_axis=3,
        tiled=True,
    )
    polarization = reorder(back, count, groups)
    first = lax.all_to_all(
        lax.all_to_all(
            polar_cols[:, :, : E // 4], "energy", split_axis=2, concat_axis=3, tiled=True
        ),
        "mom",
        split_axis=0,
        concat_axis=3,
        tiled=True,
    )
    near = reorder(first, count, groups)
    return (polarization, screen(near, coulomb, tile_block))


def solution(mesh):
    return jax.shard_map(
        shards,
        mesh=mesh,
        in_specs=(
            P("mom", None, "energy", None),
            P("mom", None, "energy", None),
            P("mom", None, None, None),
            P(),
            P(),
        ),
        out_specs=(P("mom", None, "energy", None), P("mom", None, "energy", None)),
        check_vma=False,
    )
```

profile of v0, /device:TPU:29, one launch (start us, length us, event | category | flops | bytes accessed | tf_op | source)
XLA Modules:
  0.0 1651.9 jit_solution(5967872168802620113)
XLA Ops:
  0.6 13.8 pad_maximum_fusion.11
  14.4 129.9 %copy.274 = bf16[2,2,32,65536]{2,1,0,3:T(2,128)(2,1)} copy(bf16[2,2,32,65536]{3,2,1,0:T(8,128)(2,1)} %pad_maximum_fusion.11) | data formatting | bytes 33554432 | tf_op jit(solution)/shard_map/concatenate | solution.py:127
  144.4 67.3 %reshape.507 = bf16[16,2,262144]{2,1,0:T(2,128)(2,1)} reshape(bf16[65536,2,2,32]{3,2,1,0:T(2,128)(2,1)} %bitcast.167) | data formatting | bytes 33554432
  211.7 6.5 all-to-all-start
  226.5 373.5 %all-to-all-done = bf16[16,2,262144]{2,1,0:T(2,128)(2,1)} async-done(((bf16[16,2,262144]{2,1,0:T(2,128)(2,1)}), bf16[16,2,262144]{2,1,0:T(2,128)(2,1)}, u32[]{:S(2)}, u32[]{:S(2)}) %all-to-all-start) | async-done | bytes 16777248 | tf_op jit(solution)/shard_map/all_to_all | solution.py:129
  600.0 38.6 %reshape.508 = bf16[65536,2,2,32]{3,2,1,0:T(2,128)(2,1)} reshape(bf16[16,2,262144]{2,1,0:T(2,128)(2,1)} %all-to-all-done) | data formatting | bytes 33554432
  638.6 136.6 %copy.296 = bf16[2,2,32,16,4096]{4,2,3,1,0:T(8,128)(2,1)} copy(bf16[2,2,32,16,4096]{2,1,0,4,3:T(2,128)(2,1)} %bitcast.27) | data formatting | bytes 33554432 | tf_op jit(solution)/shard_map/all_to_all | solution.py:129
  775.2 41.2 %copy.277 = bf16[2,2,512,4096]{2,1,0,3:T(2,128)(2,1)} copy(bf16[2,2,512,4096]{3,2,1,0:T(8,128)(2,1)} %bitcast.244) | data formatting | bytes 33554432 | tf_op jit(solution)/shard_map/all_to_all | solution.py:129
  816.4 20.8 %all_to_all.99 = bf16[2,2,512,4096]{2,1,0,3:T(2,128)(2,1)S(1)} all-to-all(bf16[2,2,512,4096]{2,1,0,3:T(2,128)(2,1)} %copy.277), channel_id=1, replica_groups=mesh['energy'=16,'mom'=2] {'mom'}, dimensions={3} | all-to-all | bytes 33554432 | tf_op jit(solution)/shard_map/all_to_all | solution.py:128
  837.1 11.0 copy.278
  848.2 6.0 slice_bitcast_fusion
  854.2 8.5 broadcast_in_dim.29.clone
  862.7 435.4 %while.16 = (s32[]{:T(128)}, bf16[2,2,512,2048]{3,1,0,2:T(2,128)(2,1)}, bf16[2,2,512,2048]{2,3,0,1:T(8,128)(2,1)}, bf16[2,2,512,2048]{2,3,0,1:T(8,128)(2,1)}, s3...) while((s32[]{:T(128)}, ...), condition=%wide.region_1.2_spmd, body=%wide.region_0.1_spmd.sunk | while | flops 1021673984 | bytes 86718720 | solution.py:89
  933.5 2.2 fusion.181
  1298.1 3.6 slice.487
  1301.7 51.7 %all_to_all.100 = bf16[2,2,128,2048]{3,1,0,2:T(2,128)(2,1)S(1)} all-to-all(bf16[2,2,128,2048]{3,1,0,2:T(2,128)(2,1)S(1)} %slice.487), channel_id=1, replica_groups=mesh['energy'=16,'mom'=2] {'energy'}, dimensions={2} | all-to-all | bytes 4194304 | tf_op jit(solution)/shard_map/all_to_all | solution.py:146
  1354.6 6.6 all_to_all.101
  1361.1 6.6 all-to-all-start.2
  1369.1 3.5 copy.288
  1372.6 3.2 reshape_squeeze_reshape.3
  1377.9 3.1 copy.289
  1383.7 2.3 pad_maximum_fusion.12
  1386.0 5.4 copy.290
  1391.4 4.1 reshape.489
  1395.5 162.9 %all-to-all-done.2 = bf16[2,2,512,2048]{3,1,0,2:T(2,128)(2,1)} async-done(((bf16[2,2,512,2048]{3,1,0,2:T(2,128)(2,1)}), bf16[2,2,512,2048]{3,1,0,2:T(2,128)(2,1)}, u32[]{:S(2)}, u32[]{:S(2)}) %all-to-all-start.2) | async-done | bytes 8388640 | tf_op jit(solution)/shard_map/all_to_all | solution.py:138
  1558.4 11.4 copy.346
  1569.8 13.5 all_to_all.82
  1583.3 19.3 %all_to_all.102 = bf16[2,2,32,32768]{3,2,1,0:T(8,128)(2,1)} all-to-all(bf16[2,2,32,32768]{3,2,1,0:T(8,128)(2,1)} %all_to_all.82), channel_id=1, replica_groups=mesh['energy'=16,'mom'=2] {'mom'}, dimensions={0} | all-to-all | bytes 16777216 | tf_op jit(solution)/shard_map/all_to_all | solution.py:137
  1602.6 13.1 copy.311
  1615.7 8.3 copy.345
  1624.0 16.4 copy.284
  1640.4 11.3 reshape.487
  (1143 shorter events, 421.2 us)
Async XLA Ops:
  211.7 6.5 copy-start.2
  211.7 388.3 %all-to-all-start = ((bf16[16,2,262144]{2,1,0:T(2,128)(2,1)}), bf16[16,2,262144]{2,1,0:T(2,128)(2,1)}, u32[]{:S(2)}, u32[]{:S(2)}) async-start(bf16[16,2,262144]{2,1,0:T(2,128)(2,1)} %reshape.507), calls=%async_computation | async-start | bytes 33554432 | tf_op jit(solution)/shard_map/all_to_all | solution.py:129
  877.2 1.8 copy-start
  903.6 1.8 copy-start
  930.0 1.8 copy-start
  956.4 1.8 copy-start
  982.8 1.8 copy-start
  1009.2 1.8 copy-start
  1035.6 1.8 copy-start
  1062.0 1.8 copy-start
  1088.4 1.8 copy-start
  1114.8 1.8 copy-start
  1141.2 1.8 copy-start
  1167.6 1.8 copy-start
  1194.0 1.8 copy-start
  1220.4 1.8 copy-start
  1246.8 1.8 copy-start
  1273.2 1.8 copy-start
  1361.1 6.6 copy-start.3
  1361.1 197.3 %all-to-all-start.2 = ((bf16[2,2,512,2048]{3,1,0,2:T(2,128)(2,1)}), bf16[2,2,512,2048]{3,1,0,2:T(2,128)(2,1)}, u32[]{:S(2)}, u32[]{:S(2)}) async-start(bf16[2,2,512,2048]{3,1,0,2:T(2,128)(2,1)} %get-tuple-element.205), calls=%async_computation.2 | async-start | bytes 16777216 | tf_op jit(solution)/shard_map/all_to_all | solution.py:138
  1377.9 3.4 copy-start.1
where the time goes:
time: 1670 us; the launch traced here: 1650 us
  local copies, waits for them, and re-layouts  638 us (38%)
  waiting for transfers between devices  536 us (32%)
  matrix products  207 us (12%)
  other arithmetic  131 us (8%)
  blocking collectives  98.3 us (6%)
  loops' own time  20 us (1%)
    all_to_all x1, waiting for transfers between devices, shards(): lax.all_to_all(stacked, 'energy', split_axis=3, concat_axis=2, tiled=True)  373 us
    dot_general x192, matrix products, complex_einsum(): jnp.einsum(form, table, data, precision=lax.Precision.HIGH, preferred_ele...  204 us
    all_to_all x2, local copies, waits for them, and re-layouts, shards(): lax.all_to_all(stacked, 'energy', split_axis=3, concat_axis=2, tiled=True)  178 us
    all_to_all x1, waiting for transfers between devices, shards(): lax.all_to_all(polar_cols, 'energy', split_axis=2, concat_axis=3, tiled=T...  163 us
    concatenate x1, local copies, waits for them, and re-layouts, shards(): stacked = jnp.concatenate((lesser, greater), axis=0)  130 us
    unnamed x10, local copies, waits for them, and re-layouts  120 us
    all_to_all x1, blocking collectives, shards(): lax.all_to_all(polar_cols[:, :, :E // 4], 'energy', split_axis=2, concat_...  51.7 us
    add x32, other arithmetic, correlate(): total_re + spec_left[k][0] * other_re + spec_left[k][1] * other_im  40.4 us
  transfers between devices with their start and end apart: 2, of which 2 were waited for; matrix products, arithmetic and copies ran while one was open for 2% of the time, Pallas kernels for 0%

commit v1 on v0

v1 whole, which is shorter than its diff:
```python
import functools
import math

import jax
import jax.numpy as jnp
import ml_dtypes
import numpy as np
from jax import lax
from jax.experimental import pallas as pl
from jax.experimental.pallas import tpu as pltpu
from jax.sharding import PartitionSpec as P

AXES = ("energy", "mom")
LANES = 128


def split_table(table):
    high = table.astype(np.float32).astype(ml_dtypes.bfloat16)
    low = (table - high.astype(np.float64)).astype(np.float32).astype(ml_dtypes.bfloat16)
    return high, low


@functools.lru_cache(maxsize=None)
def tables(energies, scale):
    period = 2 * energies
    turns = (2 * np.arange(energies)[:, None] + 1) * np.arange(energies)[None, :] % (2 * period)
    angle = np.pi / period * turns
    forward = np.concatenate((np.cos(angle), -np.sin(angle)), axis=0)
    backward = np.concatenate((np.cos(angle).T, -np.sin(angle).T), axis=1) * (scale / period)
    f_high, f_low = split_table(forward)
    b_high, b_low = split_table(backward)
    return np.concatenate((f_high, f_low), axis=1), np.concatenate((b_high, b_low, b_high), axis=1)


def correlate_kernel(shift, forward, backward, data, out, spectra, packed):
    blocks, count, _, _, rows, width = data.shape
    energies = blocks * rows

    def spectrum(index, carry):
        k, side, part = index // 4, index // 2 % 2, index % 2
        column = data[:, k, side, part].reshape(energies, width)
        both = jnp.concatenate((column, column), axis=0)
        spectra[index] = jnp.dot(forward[...], both, preferred_element_type=jnp.float32)
        return carry

    lax.fori_loop(0, 4 * count, spectrum, 0)
    step = 16

    def multiply(index, carry):
        row = pl.multiple_of(index * step, step)

        def load(k, side):
            base = (k * 2 + side) * 2
            a_re = spectra[base, pl.ds(row, step)]
            a_im = spectra[base, pl.ds(energies + row, step)]
            b_re = spectra[base + 1, pl.ds(row, step)]
            b_im = spectra[base + 1, pl.ds(energies + row, step)]
            return a_re - b_im, a_im + b_re, a_re + b_im, a_im - b_re

        left = [load(k, 0) for k in range(count)]
        for q in range(count):
            p_re = p_im = m_re = m_im = 0.0
            for k in range(count):
                lu_re, lu_im, lv_re, lv_im = left[k]
                ru_re, ru_im, rv_re, rv_im = load(shift[q, k], 1)
                p_re = p_re + lu_re * ru_re + lu_im * ru_im
                p_im = p_im + lu_im * ru_re - lu_re * ru_im
                m_re = m_re + lv_re * rv_re + lv_im * rv_im
                m_im = m_im + lv_im * rv_re - lv_re * rv_im
            parts = ((m_im - p_im, p_re - m_re), (p_re + m_re, p_im + m_im))
            for part in range(2):
                for half in range(2):
                    value = parts[part][half]
                    high = value.astype(jnp.bfloat16)
                    low = (value - high.astype(jnp.float32)).astype(jnp.bfloat16)
                    packed[2 * q + part, pl.ds(half * energies + row, step)] = high
                    packed[2 * q + part, pl.ds((2 + half) * energies + row, step)] = high
                    packed[2 * q + part, pl.ds((4 + half) * energies + row, step)] = low
        return carry

    lax.fori_loop(0, energies // step, multiply, 0)

    def invert(index, carry):
        result = jnp.dot(backward[...], packed[index], preferred_element_type=jnp.float32)
        out[:, index // 2, index % 2] = result.astype(jnp.bfloat16).reshape(blocks, rows, width)
        return carry

    lax.fori_loop(0, 2 * count, invert, 0)


def correlate(data, shift_table, forward, backward):
    blocks, count, _, _, rows, columns = data.shape
    energies = blocks * rows
    width = 256 if columns % 256 == 0 else columns
    work = 2 * columns * energies * energies * (16 * count + 12 * count)
    return pl.pallas_call(
        correlate_kernel,
        grid=(columns // width,),
        in_specs=[
            pl.BlockSpec(memory_space=pltpu.SMEM),
            pl.BlockSpec(forward.shape, lambda i: (0, 0)),
            pl.BlockSpec(backward.shape, lambda i: (0, 0)),
            pl.BlockSpec((blocks, count, 2, 2, rows, width), lambda i: (0, 0, 0, 0, 0, i)),
        ],
        out_specs=pl.BlockSpec((blocks, count, 2, rows, width), lambda i: (0, 0, 0, 0, i)),
        out_shape=jax.ShapeDtypeStruct((blocks, count, 2, rows, columns), jnp.bfloat16),
        scratch_shapes=[
            pltpu.VMEM((4 * count, 2 * energies, width), jnp.float32),
            pltpu.VMEM((2 * count, 6 * energies, width), jnp.bfloat16),
        ],
        compiler_params=pltpu.CompilerParams(vmem_limit_bytes=48 * 2**20),
        cost_estimate=pl.CostEstimate(
            flops=work, bytes_accessed=data.size * 3, transcendentals=0
        ),
        name="correlate",
    )(shift_table, forward, backward, data)


def pack_kernel(lesser, greater, out):
    out[0, 0] = lesser[0]
    out[0, 1] = greater[0]


def pack(lesser, greater, start, width, devices):
    _, _, rows, _ = lesser.shape
    if rows % 16 or width % LANES or start % width:
        both = jnp.concatenate((lesser, greater), axis=0)[..., start : start + devices * width]
        return jnp.transpose(both.reshape(2, 2, rows, devices, width), (3, 0, 1, 2, 4))
    base = start // width
    spec = pl.BlockSpec((1, 2, rows, width), lambda i: (0, 0, 0, base + i))
    return pl.pallas_call(
        pack_kernel,
        grid=(devices,),
        in_specs=[spec, spec],
        out_specs=pl.BlockSpec((1, 2, 2, rows, width), lambda i: (i, 0, 0, 0, 0)),
        out_shape=jax.ShapeDtypeStruct((devices, 2, 2, rows, width), jnp.bfloat16),
        name="pack",
    )(lesser, greater)


def unpack_kernel(*refs):
    refs[-1][0] = refs[0][0]


def unpack(received, start, total, result):
    devices, _, rows, width = received.shape
    base = start // width
    more = {} if result is None else {"input_output_aliases": {1: 0}}
    held = [] if result is None else [result]
    return pl.pallas_call(
        unpack_kernel,
        grid=(devices,),
        in_specs=[pl.BlockSpec((1, 2, rows, width), lambda i: (i, 0, 0, 0))]
        + [pl.BlockSpec(memory_space=pl.ANY)] * len(held),
        out_specs=pl.BlockSpec((1, 2, rows, width), lambda i: (0, 0, 0, base + i)),
        out_shape=jax.ShapeDtypeStruct((1, 2, rows, total), jnp.bfloat16),
        name="unpack",
        **more,
    )(received, *held)


def exchange(array):
    return lax.all_to_all(array, AXES, split_axis=0, concat_axis=0, tiled=True)


def after(value, *earlier):
    return lax.optimization_barrier((value, *earlier))[0]


def screen(near, coulomb, tile_block):
    tiles_n, block = coulomb.shape[1], coulomb.shape[2]
    levels = near.shape[2]
    band = (tiles_n + 2) // 3
    tiles = near.reshape(tiles_n, block, 2, levels, block)
    labels = jnp.arange(tiles_n, dtype=jnp.int32)
    onehot = tile_block[:, None] == labels[None, :]
    inverse = jnp.sum(jnp.where(onehot, labels[:, None], 0), axis=0)
    ordered = jnp.take(tiles, inverse, axis=0)
    results = []
    for r in range(band):
        for c in range(max(0, r - 1), min(band, r + 2)):
            inner = [l for l in range(max(0, r - 1), min(band, r + 2)) if abs(l - c) <= 1]
            acc = sum(
                jnp.einsum(
                    "ij,jsek->seik",
                    coulomb[0, 2 * r + l],
                    ordered[2 * l + c],
                    preferred_element_type=jnp.float32,
                )
                for l in inner
            )
            results.append(acc)
    return jnp.stack(results, axis=2).reshape(1, 2, levels, tiles_n * block * block)


def shards(lesser, greater, coulomb, tile_block, shift_table):
    count = lax.axis_size("mom")
    groups = lax.axis_size("energy")
    devices = count * groups
    rows, total = lesser.shape[2:]
    energies = rows * groups
    leading = energies // 4 // groups
    block = coulomb.shape[2]
    columns = total // devices
    chunks = 2 if columns % (2 * LANES) == 0 else 1
    width = columns // chunks
    direct = rows % 16 == 0
    forward, backward = (jnp.asarray(t) for t in tables(energies, 1.0 / math.sqrt(count * energies)))

    received, previous = [], None
    for chunk in range(chunks):
        sent = pack(lesser, greater, chunk * devices * width, width, devices)
        if previous is not None:
            sent = after(sent, previous)
        previous = exchange(sent)
        received.append(previous)

    outs, firsts, polar = [], [], None
    for chunk in range(chunks):
        data = received[chunk].reshape(groups, count, 2, 2, rows, width)
        if not direct:
            data = jnp.transpose(data, (1, 2, 3, 0, 4, 5)).reshape(1, count, 2, 2, energies, width)
        polar = correlate(data, shift_table, forward, backward)
        if not direct:
            polar = polar.reshape(count, 2, groups, rows, width)
            polar = jnp.transpose(polar, (2, 0, 1, 3, 4))
        outs.append(polar.reshape(devices, 2, rows, width))
        if leading:
            head = jnp.transpose(polar[: groups // 4], (1, 2, 0, 3, 4))
            head = head.reshape(count, 2, groups, leading, width)
            firsts.append(jnp.transpose(head, (2, 0, 1, 3, 4)).reshape(devices, 2, leading, width))

    results = []
    for chunk in range(chunks):
        if chunk == chunks - 1:
            first = jnp.concatenate(firsts, axis=3)
            first = after(first, previous)
            previous = near = exchange(first)
        previous = exchange(after(outs[chunk], previous))
        results.append(previous)

    polarization = None
    for chunk in range(chunks):
        if direct:
            polarization = unpack(results[chunk], chunk * devices * width, total, polarization)
    if not direct:
        pieces = jnp.stack(results)
        polarization = jnp.transpose(pieces, (2, 3, 0, 1, 4)).reshape(1, 2, rows, total)
    near = near.reshape(devices, 2, leading, chunks, width // block, block)
    near = jnp.transpose(near, (3, 0, 4, 1, 2, 5)).reshape(total // block, 2, leading, block)
    return (polarization, screen(near, coulomb, tile_block))


def solution(mesh):
    return jax.shard_map(
        shards,
        mesh=mesh,
        in_specs=(
            P("mom", None, "energy", None),
            P("mom", None, "energy", None),
            P("mom", None, None, None),
            P(),
            P(),
        ),
        out_specs=(P("mom", None, "energy", None), P("mom", None, "energy", None)),
        check_vma=False,
    )
```

time: 1670 us -> 672 us (0.40)
  local copies, waits for them, and re-layouts: 638 us -> 22.5 us
  matrix products: 207 us -> 2.36 us
  Pallas kernels: 0 us -> 176 us
  waiting for transfers between devices: 536 us -> 376 us
  other arithmetic: 131 us -> 5.79 us
  blocking collectives: 98.3 us -> 53 us
  loops' own time: 20 us -> 0 us
    all_to_all x6 -> x0, local copies, waits for them, and re-layouts: 215 us -> none  [the longest x2 178 us: shards(): lax.all_to_all(stacked, 'energy', split_axis=3, concat_axis=2, tiled=True)]
    dot_general x200 -> x8, matrix products: 207 us -> 2.36 us  [screen(): jnp.einsum('ij,jsek->seik', coulomb[0, 2 * r + l], ordered[2 * l + c], pr...]
    pallas_call x0 -> x6, Pallas kernels: none -> 176 us  [the longest x2 102 us: correlate(): pl.pallas_call(correlate_kernel, grid=(columns // width,), in_specs=[pl.B...]
    all_to_all x2 -> x4, waiting for transfers between devices: 536 us -> 376 us  [exchange(): return lax.all_to_all(array, AXES, split_axis=0, concat_axis=0, tiled=True)]
    concatenate x1 -> x0, local copies, waits for them, and re-layouts: 130 us -> none  [shards(): stacked = jnp.concatenate((lesser, greater), axis=0)]
    unnamed x10 -> x12, local copies, waits for them, and re-layouts: 120 us -> 3 us
    slice x146 -> x0, local copies, waits for them, and re-layouts: 51.2 us -> none  [the longest x16 22.1 us: spectrum(): pair[0].astype(jnp.float32)]
    all_to_all x4 -> x1, blocking collectives: 98.3 us -> 53 us  [exchange(): return lax.all_to_all(array, AXES, split_axis=0, concat_axis=0, tiled=True)]
  transfers between devices with their start and end apart: 2 -> 4, of which waited for: 2 -> 4; matrix products, arithmetic and copies ran while one was open for 2% -> 4% of each run, Pallas kernels for 0% -> 21%
where the time goes in v1:
time: 672 us; the launch traced here: 665 us
  waiting for transfers between devices  376 us (56%)
  Pallas kernels  176 us (26%)
  blocking collectives  53 us (8%)
  starting transfers between devices  28.9 us (4%)
  local copies, waits for them, and re-layouts  22.5 us (3%)
    all_to_all x4, waiting for transfers between devices, exchange(): return lax.all_to_all(array, AXES, split_axis=0, concat_axis=0, tiled=True)  376 us
    pallas_call x2, Pallas kernels, correlate(): pl.pallas_call(correlate_kernel, grid=(columns // width,), in_specs=[pl.B...  102 us
    all_to_all x1, blocking collectives, exchange(): return lax.all_to_all(array, AXES, split_axis=0, concat_axis=0, tiled=True)  53 us
    pallas_call x2, Pallas kernels, pack(): pl.pallas_call(pack_kernel, grid=(devices,), in_specs=[spec, spec], out_s...  39 us
    pallas_call x2, Pallas kernels, unpack(): pl.pallas_call(unpack_kernel, grid=(devices,), in_specs=[pl.BlockSpec((1,...  35.6 us
    all_to_all x4, starting transfers between devices, exchange(): return lax.all_to_all(array, AXES, split_axis=0, concat_axis=0, tiled=True)  28.9 us
  transfers between devices with their start and end apart: 4, of which 4 were waited for; matrix products, arithmetic and copies ran while one was open for 4% of the time, Pallas kernels for 21%

profile of v1, /device:TPU:29, one launch (start us, length us, event | category | flops | bytes accessed | tf_op | source)
XLA Modules:
  0.0 665.5 jit_solution(14694461469943772676)
XLA Ops:
  0.6 19.5 %pack.3 = bf16[32,2,2,32,1024]{4,3,2,1,0:T(8,128)(2,1)} custom-call(bf16[1,2,32,65536]{3,2,1,0:T(8,128)(2,1)} %lesser.3, bf16[1,2,32,65536]{3,2,1,0:T(8,128)(2,1)} %greater.3), custom_call_target="tpu_custom_call" | custom-call | tf_op jit(solution)/shard_map/pack/pallas_call | solution.py:131
  20.2 6.2 all-to-all-start
  26.4 19.5 %pack.2 = bf16[32,2,2,32,1024]{4,3,2,1,0:T(8,128)(2,1)} custom-call(bf16[1,2,32,65536]{3,2,1,0:T(8,128)(2,1)} %lesser.3, bf16[1,2,32,65536]{3,2,1,0:T(8,128)(2,1)} %greater.3), custom_call_target="tpu_custom_call" | custom-call | tf_op jit(solution)/shard_map/pack/pallas_call | solution.py:131
  45.9 161.9 %all-to-all-done = bf16[32,2,2,32,1024]{4,3,2,1,0:T(8,128)(2,1)} async-done(((bf16[32,2,2,32,1024]{4,3,2,1,0:T(8,128)(2,1)}), bf16[32,2,2,32,1024]{4,3,2,1,0:T(8,128)(2,1)}, u32[]{:S(2)}, u32[]{:S(2)}) %all-to-all-start) | async-done | bytes 8388640 | tf_op jit(solution)/shard_map/all_to_all | solution.py:163
  207.8 8.3 %all-to-all-start.1 = ((bf16[32,2,2,32,1024]{4,3,2,1,0:T(8,128)(2,1)}), bf16[32,2,2,32,1024]{4,3,2,1,0:T(8,128)(2,1)}, u32[]{:S(2)}, u32[]{:S(2)}) async-start(bf16[32,2,2,32,1024]{4,3,2,1,0:T(8,128)(2,1)} %pack.2), calls=%async_computation.1 | async-start | bytes 16777216 | tf_op jit(solution)/shard_map/all_to_all | solution.py:163
  216.2 1.6 copy-done.2
  217.7 50.9 %correlate.3 = bf16[16,2,2,32,1024]{4,3,2,1,0:T(8,128)(2,1)} custom-call(s32[2,2]{1,0:T(2,128)S(1)} %copy-done, bf16[1024,1024]{1,0:T(8,128)(2,1)S(1)} %copy-done.2, bf16[512,3072]{1,0:T(8,128)(2,1)S(1)} %copy-done.1, bf16[16,2,2,2,32,1024]{5,4,3,2,1,0:T(8,128)(2,1)} %bitcast.2.data), custom_call_target="tpu_custom_call" | custom-call | flops 30064771072 | bytes 12582912 | tf_op jit(solution)/shard_map/correlate/pallas_call | solution.py:96
  268.6 128.8 %all-to-all-done.1 = bf16[32,2,2,32,1024]{4,3,2,1,0:T(8,128)(2,1)} async-done(((bf16[32,2,2,32,1024]{4,3,2,1,0:T(8,128)(2,1)}), bf16[32,2,2,32,1024]{4,3,2,1,0:T(8,128)(2,1)}, u32[]{:S(2)}, u32[]{:S(2)}) %all-to-all-start.1) | async-done | bytes 8388640 | tf_op jit(solution)/shard_map/all_to_all | solution.py:163
  397.4 8.5 %all-to-all-start.2 = ((bf16[32,2,32,1024]{3,2,1,0:T(8,128)(2,1)}), bf16[32,2,32,1024]{3,2,1,0:T(8,128)(2,1)}, u32[]{:S(2)}, u32[]{:S(2)}) async-start(bf16[32,2,32,1024]{3,2,1,0:T(8,128)(2,1)} %bitcast.97), calls=%async_computation.2 | async-start | bytes 8388608 | tf_op jit(solution)/shard_map/all_to_all | solution.py:163
  405.9 1.3 slice_bitcast_fusion.1
  407.4 1.4 copy-done.3
  408.8 51.0 %correlate.2 = bf16[16,2,2,32,1024]{4,3,2,1,0:T(8,128)(2,1)} custom-call(s32[2,2]{1,0:T(2,128)S(1)} %copy-done, bf16[1024,1024]{1,0:T(8,128)(2,1)S(1)} %copy-done.3, bf16[512,3072]{1,0:T(8,128)(2,1)S(1)} %copy-done.1, bf16[16,2,2,2,32,1024]{5,4,3,2,1,0:T(8,128)(2,1)} %bitcast.data), custom_call_target="tpu_custom_call" | custom-call | flops 30064771072 | bytes 12582912 | tf_op jit(solution)/shard_map/correlate/pallas_call | solution.py:96
  459.8 1.3 slice_bitcast_fusion
  461.3 1.5 pad_maximum_fusion.1
  462.8 34.4 %all-to-all-done.2.refs_0_ = bf16[32,2,32,1024]{3,2,1,0:T(8,128)(2,1)} async-done(((bf16[32,2,32,1024]{3,2,1,0:T(8,128)(2,1)}), bf16[32,2,32,1024]{3,2,1,0:T(8,128)(2,1)}, u32[]{:S(2)}, u32[]{:S(2)}) %all-to-all-start.2) | async-done | bytes 4194336 | tf_op jit(solution)/shard_map/all_to_all | solution.py:163
  497.2 53.0 %all_to_all.25 = bf16[32,2,8,2048]{3,2,1,0:T(8,128)(2,1)S(1)} all-to-all(bf16[32,2,8,2048]{3,2,1,0:T(8,128)(2,1)} %pad_maximum_fusion.1), channel_id=1, replica_groups=mesh['energy'=16,'mom'=2] {'energy','mom'}, dimensions={0} | all-to-all | bytes 4194304 | tf_op jit(solution)/shard_map/all_to_all | solution.py:163
  550.2 6.0 all-to-all-start.4
  556.3 17.8 %unpack.2.refs_1_ = bf16[1,2,32,65536]{3,2,1,0:T(8,128)(2,1)} custom-call(bf16[32,2,32,1024]{3,2,1,0:T(8,128)(2,1)} %all-to-all-done.2.refs_0_), custom_call_target="tpu_custom_call" | custom-call | tf_op jit(solution)/shard_map/unpack/pallas_call | solution.py:150
  574.1 1.7 copy.21
  575.8 2.5 gather_fusion
  578.4 2.9 copy.22
  581.3 1.9 broadcast_select_fusion
  583.2 0.3 fusion.6
  583.5 0.3 fusion
  584.1 0.3 fusion.1
  584.7 0.3 fusion.2
  585.0 0.3 fusion.5
  585.6 2.3 pad_maximum_fusion
  587.9 5.4 copy.23
  593.3 4.0 reshape.62
  597.2 50.4 %all-to-all-done.4.refs_0_ = bf16[32,2,32,1024]{3,2,1,0:T(8,128)(2,1)} async-done(((bf16[32,2,32,1024]{3,2,1,0:T(8,128)(2,1)}), bf16[32,2,32,1024]{3,2,1,0:T(8,128)(2,1)}, u32[]{:S(2)}, u32[]{:S(2)}) %all-to-all-start.4) | async-done | bytes 4194336 | tf_op jit(solution)/shard_map/all_to_all | solution.py:163
  647.6 17.8 %unpack.3 = bf16[1,2,32,65536]{3,2,1,0:T(8,128)(2,1)} custom-call(bf16[32,2,32,1024]{3,2,1,0:T(8,128)(2,1)} %all-to-all-done.4.refs_0_, bf16[1,2,32,65536]{3,2,1,0:T(8,128)(2,1)} %unpack.2.refs_1_), custom_call_target="tpu_custom_call", output_to_operand_aliasing={{}: (1, {})} | custom-call | tf_op jit(solution)/shard_map/unpack/pallas_call | solution.py:150
  (21 shorter events, 1.4 us)
Async XLA Ops:
  20.2 187.6 %all-to-all-start = ((bf16[32,2,2,32,1024]{4,3,2,1,0:T(8,128)(2,1)}), bf16[32,2,2,32,1024]{4,3,2,1,0:T(8,128)(2,1)}, u32[]{:S(2)}, u32[]{:S(2)}) async-start(bf16[32,2,2,32,1024]{4,3,2,1,0:T(8,128)(2,1)} %pack.3), calls=%async_computation | async-start | bytes 16777216 | tf_op jit(solution)/shard_map/all_to_all | solution.py:163
  45.9 170.3 %copy-start = (s32[2,2]{1,0:T(2,128)S(1)}, s32[2,2]{1,0:T(2,128)}, u32[]{:S(2)}) copy-start(s32[2,2]{1,0:T(2,128)} %shift.3) | copy-start | bytes 52
  45.9 170.3 %copy-start.1 = (bf16[512,3072]{1,0:T(8,128)(2,1)S(1)}, bf16[512,3072]{1,0:T(8,128)(2,1)}, u32[]{:S(2)}) copy-start(bf16[512,3072]{1,0:T(8,128)(2,1)} %constant.22.clone.backward) | copy-start | bytes 9437188
  207.8 189.6 %all-to-all-start.1 = ((bf16[32,2,2,32,1024]{4,3,2,1,0:T(8,128)(2,1)}), bf16[32,2,2,32,1024]{4,3,2,1,0:T(8,128)(2,1)}, u32[]{:S(2)}, u32[]{:S(2)}) async-start(bf16[32,2,2,32,1024]{4,3,2,1,0:T(8,128)(2,1)} %pack.2), calls=%async_computation.1 | async-start | bytes 16777216 | tf_op jit(solution)/shard_map/all_to_all | solution.py:163
  216.1 1.6 copy-start.2
  397.4 99.8 %all-to-all-start.2 = ((bf16[32,2,32,1024]{3,2,1,0:T(8,128)(2,1)}), bf16[32,2,32,1024]{3,2,1,0:T(8,128)(2,1)}, u32[]{:S(2)}, u32[]{:S(2)}) async-start(bf16[32,2,32,1024]{3,2,1,0:T(8,128)(2,1)} %bitcast.97), calls=%async_computation.2 | async-start | bytes 8388608 | tf_op jit(solution)/shard_map/all_to_all | solution.py:163
  407.2 1.6 copy-start.3
  550.2 6.0 copy-start.5
  550.2 97.4 %all-to-all-start.4 = ((bf16[32,2,32,1024]{3,2,1,0:T(8,128)(2,1)}), bf16[32,2,32,1024]{3,2,1,0:T(8,128)(2,1)}, u32[]{:S(2)}, u32[]{:S(2)}) async-start(bf16[32,2,32,1024]{3,2,1,0:T(8,128)(2,1)} %bitcast.96), calls=%async_computation.4 | async-start | bytes 8388608 | tf_op jit(solution)/shard_map/all_to_all | solution.py:163
  581.3 1.9 copy-start.4

commit v2 on v1

--- a/solution.py
+++ b/solution.py
@@ -116,44 +116,85 @@
     )(shift_table, forward, backward, data)
 
 
-def pack_kernel(lesser, greater, out):
-    out[0, 0] = lesser[0]
-    out[0, 1] = greater[0]
+def stage(pairs, arrived, left):
+    inward = [
+        pltpu.make_async_copy(source, buffer, arrived.at[index])
+        for index, (source, buffer, _) in enumerate(pairs)
+    ]
+    outward = [
+        pltpu.make_async_copy(buffer, target, left.at[index])
+        for index, (_, buffer, target) in enumerate(pairs)
+    ]
+    for copy in inward:
+        copy.start()
+    for first, second in zip(inward, outward):
+        first.wait()
+        second.start()
+    for copy in outward:
+        copy.wait()
+
+
+def pack_kernel(start, lesser, greater, out, buffer, arrived, left):
+    devices, _, _, _, width = out.shape
+    pairs = []
+    for index in range(devices):
+        columns = pl.ds(start + index * width, width)
+        for side, array in enumerate((lesser, greater)):
+            pairs.append((array.at[0, :, :, columns], buffer.at[index, side], out.at[index, side]))
+    stage(pairs, arrived, left)
 
 
 def pack(lesser, greater, start, width, devices):
     _, _, rows, _ = lesser.shape
-    if rows % 16 or width % LANES or start % width:
+    if rows % 16 or width % LANES or devices > 64:
         both = jnp.concatenate((lesser, greater), axis=0)[..., start : start + devices * width]
         return jnp.transpose(both.reshape(2, 2, rows, devices, width), (3, 0, 1, 2, 4))
-    base = start // width
-    spec = pl.BlockSpec((1, 2, rows, width), lambda i: (0, 0, 0, base + i))
     return pl.pallas_call(
-        pack_kernel,
-        grid=(devices,),
-        in_specs=[spec, spec],
-        out_specs=pl.BlockSpec((1, 2, 2, rows, width), lambda i: (i, 0, 0, 0, 0)),
+        functools.partial(pack_kernel, start),
+        in_specs=[pl.BlockSpec(memory_space=pltpu.HBM)] * 2,
+        out_specs=pl.BlockSpec(memory_space=pltpu.HBM),
         out_shape=jax.ShapeDtypeStruct((devices, 2, 2, rows, width), jnp.bfloat16),
+        scratch_shapes=[
+            pltpu.VMEM((devices, 2, 2, rows, width), jnp.bfloat16),
+            pltpu.SemaphoreType.DMA((2 * devices,)),
+            pltpu.SemaphoreType.DMA((2 * devices,)),
+        ],
+        compiler_params=pltpu.CompilerParams(vmem_limit_bytes=48 * 2**20),
+        cost_estimate=pl.CostEstimate(
+            flops=0, bytes_accessed=devices * width * rows * 16, transcendentals=0
+        ),
         name="pack",
     )(lesser, greater)
 
 
-def unpack_kernel(*refs):
-    refs[-1][0] = refs[0][0]
+def unpack_kernel(start, *refs):
+    received, (out, buffer, arrived, left) = refs[0], refs[-4:]
+    devices, _, _, width = received.shape
+    pairs = []
+    for index in range(devices):
+        columns = pl.ds(start + index * width, width)
+        pairs.append((received.at[index], buffer.at[index], out.at[0, :, :, columns]))
+    stage(pairs, arrived, left)
 
 
 def unpack(received, start, total, result):
     devices, _, rows, width = received.shape
-    base = start // width
     more = {} if result is None else {"input_output_aliases": {1: 0}}
     held = [] if result is None else [result]
     return pl.pallas_call(
-        unpack_kernel,
-        grid=(devices,),
-        in_specs=[pl.BlockSpec((1, 2, rows, width), lambda i: (i, 0, 0, 0))]
-        + [pl.BlockSpec(memory_space=pl.ANY)] * len(held),
-        out_specs=pl.BlockSpec((1, 2, rows, width), lambda i: (0, 0, 0, base + i)),
+        functools.partial(unpack_kernel, start),
+        in_specs=[pl.BlockSpec(memory_space=pltpu.HBM)] * (1 + len(held)),
+        out_specs=pl.BlockSpec(memory_space=pltpu.HBM),
         out_shape=jax.ShapeDtypeStruct((1, 2, rows, total), jnp.bfloat16),
+        scratch_shapes=[
+            pltpu.VMEM(received.shape, jnp.bfloat16),
+            pltpu.SemaphoreType.DMA((devices,)),
+            pltpu.SemaphoreType.DMA((devices,)),
+        ],
+        compiler_params=pltpu.CompilerParams(vmem_limit_bytes=48 * 2**20),
+        cost_estimate=pl.CostEstimate(
+            flops=0, bytes_accessed=devices * width * rows * 8, transcendentals=0
+        ),
         name="unpack",
         **more,
     )(received, *held)

time: 672 us -> 645 us (0.960)
  Pallas kernels: 176 us -> 126 us
  waiting for transfers between devices: 376 us -> 401 us
    pallas_call x4, Pallas kernels: 74.6 us -> 24.4 us  [the longest x2 15.3 us: pack(): pl.pallas_call(functools.partial(pack_kernel, start), in_specs=[pl.BlockS...]
    all_to_all x4, waiting for transfers between devices: 376 us -> 401 us  [exchange(): return lax.all_to_all(array, AXES, split_axis=0, concat_axis=0, tiled=True)]
  transfers between devices with their start and end apart: 4 -> 4, of which waited for: 4 -> 4; matrix products, arithmetic and copies ran while one was open for 4% -> 4% of each run, Pallas kernels for 21% -> 18%
where the time goes in v2:
time: 645 us; the launch traced here: 640 us
  waiting for transfers between devices  401 us (62%)
  Pallas kernels  126 us (20%)
  blocking collectives  53 us (8%)
  starting transfers between devices  29 us (4%)
  local copies, waits for them, and re-layouts  22.5 us (3%)
    all_to_all x4, waiting for transfers between devices, exchange(): return lax.all_to_all(array, AXES, split_axis=0, concat_axis=0, tiled=True)  401 us
    pallas_call x2, Pallas kernels, correlate(): pl.pallas_call(correlate_kernel, grid=(columns // width,), in_specs=[pl.B...  102 us
    all_to_all x1, blocking collectives, exchange(): return lax.all_to_all(array, AXES, split_axis=0, concat_axis=0, tiled=True)  53 us
    all_to_all x4, starting transfers between devices, exchange(): return lax.all_to_all(array, AXES, split_axis=0, concat_axis=0, tiled=True)  29 us
    pallas_call x2, Pallas kernels, pack(): pl.pallas_call(functools.partial(pack_kernel, start), in_specs=[pl.BlockS...  15.3 us
  transfers between devices with their start and end apart: 4, of which 4 were waited for; matrix products, arithmetic and copies ran while one was open for 4% of the time, Pallas kernels for 18%

profile of v2, /device:TPU:29, one launch (start us, length us, event | category | flops | bytes accessed | tf_op | source)
XLA Modules:
  0.0 640.3 jit_solution(14057036385809217867)
XLA Ops:
  0.6 7.7 %pack.3 = bf16[32,2,2,32,1024]{4,3,2,1,0:T(8,128)(2,1)} custom-call(bf16[1,2,32,65536]{3,2,1,0:T(8,128)(2,1)} %lesser.3, bf16[1,2,32,65536]{3,2,1,0:T(8,128)(2,1)} %greater.3), custom_call_target="tpu_custom_call" | custom-call | bytes 16777216 | tf_op jit(solution)/shard_map/pack/pallas_call | solution.py:152
  8.3 6.2 all-to-all-start
  14.6 7.6 %pack.2 = bf16[32,2,2,32,1024]{4,3,2,1,0:T(8,128)(2,1)} custom-call(bf16[1,2,32,65536]{3,2,1,0:T(8,128)(2,1)} %lesser.3, bf16[1,2,32,65536]{3,2,1,0:T(8,128)(2,1)} %greater.3), custom_call_target="tpu_custom_call" | custom-call | bytes 16777216 | tf_op jit(solution)/shard_map/pack/pallas_call | solution.py:152
  22.2 173.7 %all-to-all-done = bf16[32,2,2,32,1024]{4,3,2,1,0:T(8,128)(2,1)} async-done(((bf16[32,2,2,32,1024]{4,3,2,1,0:T(8,128)(2,1)}), bf16[32,2,2,32,1024]{4,3,2,1,0:T(8,128)(2,1)}, u32[]{:S(2)}, u32[]{:S(2)}) %all-to-all-start) | async-done | bytes 8388640 | tf_op jit(solution)/shard_map/all_to_all | solution.py:204
  196.0 8.3 %all-to-all-start.1 = ((bf16[32,2,2,32,1024]{4,3,2,1,0:T(8,128)(2,1)}), bf16[32,2,2,32,1024]{4,3,2,1,0:T(8,128)(2,1)}, u32[]{:S(2)}, u32[]{:S(2)}) async-start(bf16[32,2,2,32,1024]{4,3,2,1,0:T(8,128)(2,1)} %pack.2), calls=%async_computation.1 | async-start | bytes 16777216 | tf_op jit(solution)/shard_map/all_to_all | solution.py:204
  204.3 1.6 copy-done.2
  205.9 50.9 %correlate.3 = bf16[16,2,2,32,1024]{4,3,2,1,0:T(8,128)(2,1)} custom-call(s32[2,2]{1,0:T(2,128)S(1)} %copy-done, bf16[1024,1024]{1,0:T(8,128)(2,1)S(1)} %copy-done.2, bf16[512,3072]{1,0:T(8,128)(2,1)S(1)} %copy-done.1, bf16[16,2,2,2,32,1024]{5,4,3,2,1,0:T(8,128)(2,1)} %bitcast.2.data), custom_call_target="tpu_custom_call" | custom-call | flops 30064771072 | bytes 12582912 | tf_op jit(solution)/shard_map/correlate/pallas_call | solution.py:96
  256.8 128.8 %all-to-all-done.1 = bf16[32,2,2,32,1024]{4,3,2,1,0:T(8,128)(2,1)} async-done(((bf16[32,2,2,32,1024]{4,3,2,1,0:T(8,128)(2,1)}), bf16[32,2,2,32,1024]{4,3,2,1,0:T(8,128)(2,1)}, u32[]{:S(2)}, u32[]{:S(2)}) %all-to-all-start.1) | async-done | bytes 8388640 | tf_op jit(solution)/shard_map/all_to_all | solution.py:204
  385.6 8.5 %all-to-all-start.2 = ((bf16[32,2,32,1024]{3,2,1,0:T(8,128)(2,1)}), bf16[32,2,32,1024]{3,2,1,0:T(8,128)(2,1)}, u32[]{:S(2)}, u32[]{:S(2)}) async-start(bf16[32,2,32,1024]{3,2,1,0:T(8,128)(2,1)} %bitcast.97), calls=%async_computation.2 | async-start | bytes 8388608 | tf_op jit(solution)/shard_map/all_to_all | solution.py:204
  394.0 1.3 slice_bitcast_fusion.1
  395.6 1.4 copy-done.3
  397.0 50.9 %correlate.2 = bf16[16,2,2,32,1024]{4,3,2,1,0:T(8,128)(2,1)} custom-call(s32[2,2]{1,0:T(2,128)S(1)} %copy-done, bf16[1024,1024]{1,0:T(8,128)(2,1)S(1)} %copy-done.3, bf16[512,3072]{1,0:T(8,128)(2,1)S(1)} %copy-done.1, bf16[16,2,2,2,32,1024]{5,4,3,2,1,0:T(8,128)(2,1)} %bitcast.data), custom_call_target="tpu_custom_call" | custom-call | flops 30064771072 | bytes 12582912 | tf_op jit(solution)/shard_map/correlate/pallas_call | solution.py:96
  447.9 1.3 slice_bitcast_fusion
  449.4 1.5 pad_maximum_fusion.1
  450.9 34.4 %all-to-all-done.2.refs_0_ = bf16[32,2,32,1024]{3,2,1,0:T(8,128)(2,1)} async-done(((bf16[32,2,32,1024]{3,2,1,0:T(8,128)(2,1)}), bf16[32,2,32,1024]{3,2,1,0:T(8,128)(2,1)}, u32[]{:S(2)}, u32[]{:S(2)}) %all-to-all-start.2) | async-done | bytes 4194336 | tf_op jit(solution)/shard_map/all_to_all | solution.py:204
  485.4 53.0 %all_to_all.25 = bf16[32,2,8,2048]{3,2,1,0:T(8,128)(2,1)S(1)} all-to-all(bf16[32,2,8,2048]{3,2,1,0:T(8,128)(2,1)} %pad_maximum_fusion.1), channel_id=1, replica_groups=mesh['energy'=16,'mom'=2] {'energy','mom'}, dimensions={0} | all-to-all | bytes 4194304 | tf_op jit(solution)/shard_map/all_to_all | solution.py:204
  538.4 6.0 all-to-all-start.4
  544.5 4.5 unpack.2.refs_1_
  549.0 1.7 copy.21
  550.7 2.5 gather_fusion
  553.3 2.9 copy.22
  556.2 1.9 broadcast_select_fusion
  558.1 0.3 fusion.6
  558.4 0.3 fusion
  559.0 0.3 fusion.1
  559.5 0.3 fusion.2
  560.1 0.3 fusion.3
  560.4 2.3 pad_maximum_fusion
  562.7 5.4 copy.23
  568.1 4.0 reshape.62
  572.1 63.7 %all-to-all-done.4.refs_0_ = bf16[32,2,32,1024]{3,2,1,0:T(8,128)(2,1)} async-done(((bf16[32,2,32,1024]{3,2,1,0:T(8,128)(2,1)}), bf16[32,2,32,1024]{3,2,1,0:T(8,128)(2,1)}, u32[]{:S(2)}, u32[]{:S(2)}) %all-to-all-start.4) | async-done | bytes 4194336 | tf_op jit(solution)/shard_map/all_to_all | solution.py:204
  635.8 4.5 unpack.3
  (21 shorter events, 1.4 us)
Async XLA Ops:
  8.3 187.6 %all-to-all-start = ((bf16[32,2,2,32,1024]{4,3,2,1,0:T(8,128)(2,1)}), bf16[32,2,2,32,1024]{4,3,2,1,0:T(8,128)(2,1)}, u32[]{:S(2)}, u32[]{:S(2)}) async-start(bf16[32,2,2,32,1024]{4,3,2,1,0:T(8,128)(2,1)} %pack.3), calls=%async_computation | async-start | bytes 16777216 | tf_op jit(solution)/shard_map/all_to_all | solution.py:204
  22.2 182.1 %copy-start = (s32[2,2]{1,0:T(2,128)S(1)}, s32[2,2]{1,0:T(2,128)}, u32[]{:S(2)}) copy-start(s32[2,2]{1,0:T(2,128)} %shift.3) | copy-start | bytes 52
  22.2 182.1 %copy-start.1 = (bf16[512,3072]{1,0:T(8,128)(2,1)S(1)}, bf16[512,3072]{1,0:T(8,128)(2,1)}, u32[]{:S(2)}) copy-start(bf16[512,3072]{1,0:T(8,128)(2,1)} %constant.22.clone.backward) | copy-start | bytes 9437188
  196.0 189.6 %all-to-all-start.1 = ((bf16[32,2,2,32,1024]{4,3,2,1,0:T(8,128)(2,1)}), bf16[32,2,2,32,1024]{4,3,2,1,0:T(8,128)(2,1)}, u32[]{:S(2)}, u32[]{:S(2)}) async-start(bf16[32,2,2,32,1024]{4,3,2,1,0:T(8,128)(2,1)} %pack.2), calls=%async_computation.1 | async-start | bytes 16777216 | tf_op jit(solution)/shard_map/all_to_all | solution.py:204
  204.3 1.6 copy-start.2
  385.6 99.8 %all-to-all-start.2 = ((bf16[32,2,32,1024]{3,2,1,0:T(8,128)(2,1)}), bf16[32,2,32,1024]{3,2,1,0:T(8,128)(2,1)}, u32[]{:S(2)}, u32[]{:S(2)}) async-start(bf16[32,2,32,1024]{3,2,1,0:T(8,128)(2,1)} %bitcast.97), calls=%async_computation.2 | async-start | bytes 8388608 | tf_op jit(solution)/shard_map/all_to_all | solution.py:204
  395.4 1.6 copy-start.3
  538.4 6.0 copy-start.5
  538.4 97.4 %all-to-all-start.4 = ((bf16[32,2,32,1024]{3,2,1,0:T(8,128)(2,1)}), bf16[32,2,32,1024]{3,2,1,0:T(8,128)(2,1)}, u32[]{:S(2)}, u32[]{:S(2)}) async-start(bf16[32,2,32,1024]{3,2,1,0:T(8,128)(2,1)} %bitcast.96), calls=%async_computation.4 | async-start | bytes 8388608 | tf_op jit(solution)/shard_map/all_to_all | solution.py:204
  556.2 1.9 copy-start.4

commit v3 on v2

--- a/solution.py
+++ b/solution.py
@@ -12,6 +12,7 @@
 
 AXES = ("energy", "mom")
 LANES = 128
+FIRST = 3
 
 
 def split_table(table):
@@ -234,6 +235,14 @@
     return jnp.stack(results, axis=2).reshape(1, 2, levels, tiles_n * block * block)
 
 
+def chunk_widths(columns):
+    step = 2 * LANES
+    if columns % step or columns < 2 * step:
+        return [columns] if columns % (2 * LANES) else [columns // 2] * 2
+    first = columns // step * FIRST // 8 * step
+    return [first, columns - first]
+
+
 def shards(lesser, greater, coulomb, tile_block, shift_table):
     count = lax.axis_size("mom")
     groups = lax.axis_size("energy")
@@ -243,22 +252,22 @@
     leading = energies // 4 // groups
     block = coulomb.shape[2]
     columns = total // devices
-    chunks = 2 if columns % (2 * LANES) == 0 else 1
-    width = columns // chunks
+    widths = chunk_widths(columns)
+    starts = [devices * sum(widths[:chunk]) for chunk in range(len(widths))]
     direct = rows % 16 == 0
     forward, backward = (jnp.asarray(t) for t in tables(energies, 1.0 / math.sqrt(count * energies)))
 
     received, previous = [], None
-    for chunk in range(chunks):
-        sent = pack(lesser, greater, chunk * devices * width, width, devices)
+    for start, width in zip(starts, widths):
+        sent = pack(lesser, greater, start, width, devices)
         if previous is not None:
             sent = after(sent, previous)
         previous = exchange(sent)
         received.append(previous)
 
-    outs, firsts, polar = [], [], None
-    for chunk in range(chunks):
-        data = received[chunk].reshape(groups, count, 2, 2, rows, width)
+    outs, firsts = [], []
+    for data, width in zip(received, widths):
+        data = data.reshape(groups, count, 2, 2, rows, width)
         if not direct:
             data = jnp.transpose(data, (1, 2, 3, 0, 4, 5)).reshape(1, count, 2, 2, energies, width)
         polar = correlate(data, shift_table, forward, backward)
@@ -266,30 +275,30 @@
             polar = polar.reshape(count, 2, groups, rows, width)
             polar = jnp.transpose(polar, (2, 0, 1, 3, 4))
         outs.append(polar.reshape(devices, 2, rows, width))
-        if leading:
-            head = jnp.transpose(polar[: groups // 4], (1, 2, 0, 3, 4))
-            head = head.reshape(count, 2, groups, leading, width)
-            firsts.append(jnp.transpose(head, (2, 0, 1, 3, 4)).reshape(devices, 2, leading, width))
+        head = jnp.transpose(polar[: groups // 4], (1, 2, 0, 3, 4))
+        head = head.reshape(count, 2, groups, leading, width)
+        firsts.append(jnp.transpose(head, (2, 0, 1, 3, 4)).reshape(devices, 2, leading, width))
 
     results = []
-    for chunk in range(chunks):
-        if chunk == chunks - 1:
-            first = jnp.concatenate(firsts, axis=3)
-            first = after(first, previous)
-            previous = near = exchange(first)
-        previous = exchange(after(outs[chunk], previous))
+    for chunk, out in enumerate(outs):
+        if chunk == len(outs) - 1:
+            previous = first = exchange(after(jnp.concatenate(firsts, axis=3), previous))
+        previous = exchange(after(out, previous))
         results.append(previous)
 
     polarization = None
-    for chunk in range(chunks):
+    for result, start in zip(results, starts):
         if direct:
-            polarization = unpack(results[chunk], chunk * devices * width, total, polarization)
+            polarization = unpack(result, start, total, polarization)
     if not direct:
-        pieces = jnp.stack(results)
-        polarization = jnp.transpose(pieces, (2, 3, 0, 1, 4)).reshape(1, 2, rows, total)
-    near = near.reshape(devices, 2, leading, chunks, width // block, block)
-    near = jnp.transpose(near, (3, 0, 4, 1, 2, 5)).reshape(total // block, 2, leading, block)
-    return (polarization, screen(near, coulomb, tile_block))
+        pieces = [jnp.transpose(result, (1, 2, 0, 3)).reshape(2, rows, -1) for result in results]
+        polarization = jnp.concatenate(pieces, axis=2)[None]
+    near = []
+    for chunk, width in enumerate(widths):
+        part = first[..., sum(widths[:chunk]) : sum(widths[: chunk + 1])]
+        part = part.reshape(devices, 2, leading, width // block, block)
+        near.append(jnp.transpose(part, (0, 3, 1, 2, 4)).reshape(-1, 2, leading, block))
+    return (polarization, screen(jnp.concatenate(near), coulomb, tile_block))
 
 
 def solution(mesh):

time: 645 us -> 644 us (level)
  transfers between devices with their start and end apart: 4 -> 4, of which waited for: 4 -> 3; matrix products, arithmetic and copies ran while one was open for 4% -> 4% of each run, Pallas kernels for 18% -> 18%
where the time goes in v3:
time: 644 us; the launch traced here: 639 us
  waiting for transfers between devices  399 us (62%)
  Pallas kernels  128 us (20%)
  blocking collectives  52.4 us (8%)
  starting transfers between devices  28.6 us (4%)
  local copies, waits for them, and re-layouts  23.1 us (4%)
    all_to_all x4, waiting for transfers between devices, exchange(): return lax.all_to_all(array, AXES, split_axis=0, concat_axis=0, tiled=True)  399 us
    pallas_call x2, Pallas kernels, correlate(): pl.pallas_call(correlate_kernel, grid=(columns // width,), in_specs=[pl.B...  102 us
    all_to_all x1, blocking collectives, exchange(): return lax.all_to_all(array, AXES, split_axis=0, concat_axis=0, tiled=True)  52.4 us
    all_to_all x4, starting transfers between devices, exchange(): return lax.all_to_all(array, AXES, split_axis=0, concat_axis=0, tiled=True)  28.6 us
    pallas_call x2, Pallas kernels, pack(): pl.pallas_call(functools.partial(pack_kernel, start), in_specs=[pl.BlockS...  15.4 us
  transfers between devices with their start and end apart: 4, of which 3 were waited for; matrix products, arithmetic and copies ran while one was open for 4% of the time, Pallas kernels for 18%

profile of v3, /device:TPU:29, one launch (start us, length us, event | category | flops | bytes accessed | tf_op | source)
XLA Modules:
  0.0 639.4 jit_solution(15333335299344210348)
XLA Ops:
  0.6 6.3 pack.3
  6.9 6.2 all-to-all-start
  13.1 9.1 %pack.2 = bf16[32,2,2,32,1280]{4,3,2,1,0:T(8,128)(2,1)} custom-call(bf16[1,2,32,65536]{3,2,1,0:T(8,128)(2,1)} %lesser.3, bf16[1,2,32,65536]{3,2,1,0:T(8,128)(2,1)} %greater.3), custom_call_target="tpu_custom_call" | custom-call | bytes 20971520 | tf_op jit(solution)/shard_map/pack/pallas_call | solution.py:153
  22.3 127.2 %all-to-all-done = bf16[32,2,2,32,768]{4,3,2,1,0:T(8,128)(2,1)} async-done(((bf16[32,2,2,32,768]{4,3,2,1,0:T(8,128)(2,1)}), bf16[32,2,2,32,768]{4,3,2,1,0:T(8,128)(2,1)}, u32[]{:S(2)}, u32[]{:S(2)}) %all-to-all-start) | async-done | bytes 6291488 | tf_op jit(solution)/shard_map/all_to_all | solution.py:205
  149.5 7.3 %all-to-all-start.1 = ((bf16[32,2,2,32,1280]{4,3,2,1,0:T(8,128)(2,1)}), bf16[32,2,2,32,1280]{4,3,2,1,0:T(8,128)(2,1)}, u32[]{:S(2)}, u32[]{:S(2)}) async-start(bf16[32,2,2,32,1280]{4,3,2,1,0:T(8,128)(2,1)} %pack.2), calls=%async_computation.1 | async-start | bytes 20971520 | tf_op jit(solution)/shard_map/all_to_all | solution.py:205
  156.9 38.9 %correlate.3 = bf16[16,2,2,32,768]{4,3,2,1,0:T(8,128)(2,1)S(1)} custom-call(s32[2,2]{1,0:T(2,128)S(1)} %copy-done.1, bf16[1024,1024]{1,0:T(8,128)(2,1)S(1)} %copy-done.3, bf16[512,3072]{1,0:T(8,128)(2,1)} %constant.22.clone.backward, bf16[16,2,2,2,32,768]{5,4,3,2,1,0:T(8,128)(2,1)} %bitcast.2.data), custom_call_target="tpu_custom_call" | custom-call | flops 22548578304 | bytes 9437184 | tf_op jit(solution)/shard_map/correlate/pallas_call | solution.py:97
  195.8 1.7 copy-done
  197.4 185.7 %all-to-all-done.1 = bf16[32,2,2,32,1280]{4,3,2,1,0:T(8,128)(2,1)} async-done(((bf16[32,2,2,32,1280]{4,3,2,1,0:T(8,128)(2,1)}), bf16[32,2,2,32,1280]{4,3,2,1,0:T(8,128)(2,1)}, u32[]{:S(2)}, u32[]{:S(2)}) %all-to-all-start.1) | async-done | bytes 10485792 | tf_op jit(solution)/shard_map/all_to_all | solution.py:205
  383.1 9.1 %all-to-all-start.2 = ((bf16[32,2,32,768]{3,2,1,0:T(8,128)(2,1)}), bf16[32,2,32,768]{3,2,1,0:T(8,128)(2,1)S(1)}, u32[]{:S(2)}, u32[]{:S(2)}) async-start(bf16[32,2,32,768]{3,2,1,0:T(8,128)(2,1)} %bitcast.101), calls=%async_computation.2 | async-start | bytes 6291456 | tf_op jit(solution)/shard_map/all_to_all | solution.py:205
  392.2 1.3 slice_bitcast_fusion.3
  393.7 0.6 copy-done.2
  394.3 1.6 copy-done.4
  395.9 62.7 %correlate.2 = bf16[16,2,2,32,1280]{4,3,2,1,0:T(8,128)(2,1)} custom-call(s32[2,2]{1,0:T(2,128)S(1)} %copy-done.1, bf16[1024,1024]{1,0:T(8,128)(2,1)S(1)} %copy-done.4, bf16[512,3072]{1,0:T(8,128)(2,1)S(1)} %copy-done.2, bf16[16,2,2,2,32,1280]{5,4,3,2,1,0:T(8,128)(2,1)} %bitcast.data), custom_call_target="tpu_custom_call" | custom-call | flops 37580963840 | bytes 15728640 | tf_op jit(solution)/shard_map/correlate/pallas_call | solution.py:97
  458.6 1.4 slice_bitcast_fusion.1
  460.3 1.6 pad_maximum_fusion.1
  461.9 52.4 %all_to_all.25 = bf16[32,2,8,2048]{3,2,1,0:T(8,128)(2,1)} all-to-all(bf16[32,2,8,2048]{3,2,1,0:T(8,128)(2,1)} %pad_maximum_fusion.1), channel_id=1, replica_groups=mesh['energy'=16,'mom'=2] {'energy','mom'}, dimensions={0} | all-to-all | bytes 4194304 | tf_op jit(solution)/shard_map/all_to_all | solution.py:205
  514.3 5.9 all-to-all-start.4
  520.4 6.3 unpack.2.refs_1_
  527.5 2.1 gather_fusion
  529.6 3.4 copy.24
  533.3 0.6 copy-done.6
  534.2 0.3 fusion
  534.8 0.3 fusion.1
  535.1 0.3 fusion.7
  535.4 0.3 fusion.2
  535.7 0.3 fusion.5
  536.0 0.3 fusion.3
  536.3 2.3 pad_maximum_fusion
  538.6 5.4 copy.25
  544.0 4.0 reshape.78
  548.0 86.2 %all-to-all-done.4.refs_0_ = bf16[32,2,32,1280]{3,2,1,0:T(8,128)(2,1)} async-done(((bf16[32,2,32,1280]{3,2,1,0:T(8,128)(2,1)}), bf16[32,2,32,1280]{3,2,1,0:T(8,128)(2,1)}, u32[]{:S(2)}, u32[]{:S(2)}) %all-to-all-start.4) | async-done | bytes 5242912 | tf_op jit(solution)/shard_map/all_to_all | solution.py:205
  634.2 5.2 unpack.3
  (29 shorter events, 2.1 us)
Async XLA Ops:
  6.9 142.6 %all-to-all-start = ((bf16[32,2,2,32,768]{4,3,2,1,0:T(8,128)(2,1)}), bf16[32,2,2,32,768]{4,3,2,1,0:T(8,128)(2,1)}, u32[]{:S(2)}, u32[]{:S(2)}) async-start(bf16[32,2,2,32,768]{4,3,2,1,0:T(8,128)(2,1)} %pack.3), calls=%async_computation | async-start | bytes 12582912 | tf_op jit(solution)/shard_map/all_to_all | solution.py:205
  22.3 134.6 %copy-start.1 = (s32[2,2]{1,0:T(2,128)S(1)}, s32[2,2]{1,0:T(2,128)}, u32[]{:S(2)}) copy-start(s32[2,2]{1,0:T(2,128)} %shift.3) | copy-start | bytes 52
  22.3 134.6 %copy-start.3 = (bf16[1024,1024]{1,0:T(8,128)(2,1)S(1)}, bf16[1024,1024]{1,0:T(8,128)(2,1)}, u32[]{:S(2)}) copy-start(bf16[1024,1024]{1,0:T(8,128)(2,1)} %constant.21.clone.forward) | copy-start | bytes 6291460
  149.5 233.6 %all-to-all-start.1 = ((bf16[32,2,2,32,1280]{4,3,2,1,0:T(8,128)(2,1)}), bf16[32,2,2,32,1280]{4,3,2,1,0:T(8,128)(2,1)}, u32[]{:S(2)}, u32[]{:S(2)}) async-start(bf16[32,2,2,32,1280]{4,3,2,1,0:T(8,128)(2,1)} %pack.2), calls=%async_computation.1 | async-start | bytes 20971520 | tf_op jit(solution)/shard_map/all_to_all | solution.py:205
  195.8 1.7 copy-start
  383.1 78.8 %all-to-all-start.2 = ((bf16[32,2,32,768]{3,2,1,0:T(8,128)(2,1)}), bf16[32,2,32,768]{3,2,1,0:T(8,128)(2,1)S(1)}, u32[]{:S(2)}, u32[]{:S(2)}) async-start(bf16[32,2,32,768]{3,2,1,0:T(8,128)(2,1)} %bitcast.101), calls=%async_computation.2 | async-start | bytes 6291456 | tf_op jit(solution)/shard_map/all_to_all | solution.py:205
  392.2 2.1 copy-start.2
  394.3 1.6 copy-start.4
  514.3 6.0 copy-start.7
  514.3 119.9 %all-to-all-start.4 = ((bf16[32,2,32,1280]{3,2,1,0:T(8,128)(2,1)}), bf16[32,2,32,1280]{3,2,1,0:T(8,128)(2,1)}, u32[]{:S(2)}, u32[]{:S(2)}) async-start(bf16[32,2,32,1280]{3,2,1,0:T(8,128)(2,1)} %bitcast.103), calls=%async_computation.4 | async-start | bytes 10485760 | tf_op jit(solution)/shard_map/all_to_all | solution.py:205
  520.4 6.3 copy-start.5
  533.0 0.9 copy-start.6

commit v4 on v3

--- a/solution.py
+++ b/solution.py
@@ -12,7 +12,7 @@
 
 AXES = ("energy", "mom")
 LANES = 128
-FIRST = 3
+FIRST = 4
 
 
 def split_table(table):
@@ -168,27 +168,28 @@
     )(lesser, greater)
 
 
-def unpack_kernel(start, *refs):
+def unpack_kernel(start, stride, offset, *refs):
     received, (out, buffer, arrived, left) = refs[0], refs[-4:]
-    devices, _, _, width = received.shape
+    devices, _, rows, width = buffer.shape
     pairs = []
     for index in range(devices):
-        columns = pl.ds(start + index * width, width)
-        pairs.append((received.at[index], buffer.at[index], out.at[0, :, :, columns]))
+        columns = pl.ds(start + index * stride + offset, width)
+        source = received.at[index, :, pl.ds(0, rows)]
+        pairs.append((source, buffer.at[index], out.at[0, :, :, columns]))
     stage(pairs, arrived, left)
 
 
-def unpack(received, start, total, result):
-    devices, _, rows, width = received.shape
+def unpack(received, rows, start, stride, offset, total, result):
+    devices, _, _, width = received.shape
     more = {} if result is None else {"input_output_aliases": {1: 0}}
     held = [] if result is None else [result]
     return pl.pallas_call(
-        functools.partial(unpack_kernel, start),
+        functools.partial(unpack_kernel, start, stride, offset),
         in_specs=[pl.BlockSpec(memory_space=pltpu.HBM)] * (1 + len(held)),
         out_specs=pl.BlockSpec(memory_space=pltpu.HBM),
         out_shape=jax.ShapeDtypeStruct((1, 2, rows, total), jnp.bfloat16),
         scratch_shapes=[
-            pltpu.VMEM(received.shape, jnp.bfloat16),
+            pltpu.VMEM((devices, 2, rows, width), jnp.bfloat16),
             pltpu.SemaphoreType.DMA((devices,)),
             pltpu.SemaphoreType.DMA((devices,)),
         ],
@@ -280,17 +281,35 @@
         firsts.append(jnp.transpose(head, (2, 0, 1, 3, 4)).reshape(devices, 2, leading, width))
 
     results = []
+    half = widths[-1] // 2
+    merge = direct and half % LANES == 0 and columns % half == 0
     for chunk, out in enumerate(outs):
         if chunk == len(outs) - 1:
-            previous = first = exchange(after(jnp.concatenate(firsts, axis=3), previous))
+            first = jnp.concatenate(firsts, axis=3)
+            if merge:
+                first = first.reshape(devices, 2, leading, columns // half, half)
+                first = jnp.transpose(first, (0, 1, 3, 2, 4)).reshape(devices, 2, -1, half)
+                first = jnp.concatenate((out[..., :half], first), axis=2)
+            previous = first = exchange(after(first, previous))
+            if merge:
+                results.append(first)
+                first = first[:, :, rows:].reshape(devices, 2, columns // half, leading, half)
+                first = jnp.transpose(first, (0, 1, 3, 2, 4)).reshape(devices, 2, leading, columns)
+                out = out[..., half:]
         previous = exchange(after(out, previous))
         results.append(previous)
 
     polarization = None
-    for result, start in zip(results, starts):
-        if direct:
-            polarization = unpack(result, start, total, polarization)
-    if not direct:
+    if direct:
+        step = 0
+        for chunk, result in enumerate(results):
+            last = chunk >= len(widths) - 1
+            polarization = unpack(
+                result, rows, starts[min(chunk, len(widths) - 1)], widths[min(chunk, len(widths) - 1)],
+                step, total, polarization,
+            )
+            step += result.shape[3] if last else 0
+    else:
         pieces = [jnp.transpose(result, (1, 2, 0, 3)).reshape(2, rows, -1) for result in results]
         polarization = jnp.concatenate(pieces, axis=2)[None]
     near = []

time: 644 us -> 643 us (level)
  waiting for transfers between devices: 399 us -> 338 us
  blocking collectives: 52.4 us -> 98.1 us
  local copies, waits for them, and re-layouts: 23.1 us -> 34.9 us
    all_to_all x4, waiting for transfers between devices: 399 us -> 338 us  [exchange(): return lax.all_to_all(array, AXES, split_axis=0, concat_axis=0, tiled=True)]
    all_to_all x1, blocking collectives: 52.4 us -> 98.1 us  [exchange(): return lax.all_to_all(array, AXES, split_axis=0, concat_axis=0, tiled=True)]
  transfers between devices with their start and end apart: 4 -> 4, of which waited for: 3 -> 4; matrix products, arithmetic and copies ran while one was open for 4% -> 6% of each run, Pallas kernels for 18% -> 18%
where the time goes in v4:
time: 643 us; the launch traced here: 639 us
  waiting for transfers between devices  338 us (53%)
  Pallas kernels  127 us (20%)
  blocking collectives  98.1 us (15%)
  local copies, waits for them, and re-layouts  34.9 us (5%)
  starting transfers between devices  29 us (5%)
  other arithmetic  7.55 us (1%)
    all_to_all x4, waiting for transfers between devices, exchange(): return lax.all_to_all(array, AXES, split_axis=0, concat_axis=0, tiled=True)  338 us
    pallas_call x2, Pallas kernels, correlate(): pl.pallas_call(correlate_kernel, grid=(columns // width,), in_specs=[pl.B...  102 us
    all_to_all x1, blocking collectives, exchange(): return lax.all_to_all(array, AXES, split_axis=0, concat_axis=0, tiled=True)  98.1 us
    all_to_all x4, starting transfers between devices, exchange(): return lax.all_to_all(array, AXES, split_axis=0, concat_axis=0, tiled=True)  29 us
    pallas_call x2, Pallas kernels, pack(): pl.pallas_call(functools.partial(pack_kernel, start), in_specs=[pl.BlockS...  15.3 us
  transfers between devices with their start and end apart: 4, of which 4 were waited for; matrix products, arithmetic and copies ran while one was open for 6% of the time, Pallas kernels for 18%

profile of v4, /device:TPU:29, one launch (start us, length us, event | category | flops | bytes accessed | tf_op | source)
XLA Modules:
  0.0 638.8 jit_solution(851796645316032133)
XLA Ops:
  0.6 7.6 %pack.3 = bf16[32,2,2,32,1024]{4,3,2,1,0:T(8,128)(2,1)} custom-call(bf16[1,2,32,65536]{3,2,1,0:T(8,128)(2,1)} %lesser.3, bf16[1,2,32,65536]{3,2,1,0:T(8,128)(2,1)} %greater.3), custom_call_target="tpu_custom_call" | custom-call | bytes 16777216 | tf_op jit(solution)/shard_map/pack/pallas_call | solution.py:153
  8.3 6.2 all-to-all-start
  14.5 7.6 %pack.2 = bf16[32,2,2,32,1024]{4,3,2,1,0:T(8,128)(2,1)} custom-call(bf16[1,2,32,65536]{3,2,1,0:T(8,128)(2,1)} %lesser.3, bf16[1,2,32,65536]{3,2,1,0:T(8,128)(2,1)} %greater.3), custom_call_target="tpu_custom_call" | custom-call | bytes 16777216 | tf_op jit(solution)/shard_map/pack/pallas_call | solution.py:153
  22.2 173.7 %all-to-all-done = bf16[32,2,2,32,1024]{4,3,2,1,0:T(8,128)(2,1)} async-done(((bf16[32,2,2,32,1024]{4,3,2,1,0:T(8,128)(2,1)}), bf16[32,2,2,32,1024]{4,3,2,1,0:T(8,128)(2,1)}, u32[]{:S(2)}, u32[]{:S(2)}) %all-to-all-start) | async-done | bytes 8388640 | tf_op jit(solution)/shard_map/all_to_all | solution.py:206
  195.9 8.3 %all-to-all-start.1 = ((bf16[32,2,2,32,1024]{4,3,2,1,0:T(8,128)(2,1)}), bf16[32,2,2,32,1024]{4,3,2,1,0:T(8,128)(2,1)}, u32[]{:S(2)}, u32[]{:S(2)}) async-start(bf16[32,2,2,32,1024]{4,3,2,1,0:T(8,128)(2,1)} %pack.2), calls=%async_computation.1 | async-start | bytes 16777216 | tf_op jit(solution)/shard_map/all_to_all | solution.py:206
  204.3 1.6 copy-done.3
  205.9 50.9 %correlate.3 = bf16[16,2,2,32,1024]{4,3,2,1,0:T(8,128)(2,1)} custom-call(s32[2,2]{1,0:T(2,128)S(1)} %copy-done.1, bf16[1024,1024]{1,0:T(8,128)(2,1)S(1)} %copy-done.3, bf16[512,3072]{1,0:T(8,128)(2,1)S(1)} %copy-done.2, bf16[16,2,2,2,32,1024]{5,4,3,2,1,0:T(8,128)(2,1)} %bitcast.2.data), custom_call_target="tpu_custom_call" | custom-call | flops 30064771072 | bytes 12582912 | tf_op jit(solution)/shard_map/correlate/pallas_call | solution.py:97
  256.7 128.8 %all-to-all-done.1 = bf16[32,2,2,32,1024]{4,3,2,1,0:T(8,128)(2,1)} async-done(((bf16[32,2,2,32,1024]{4,3,2,1,0:T(8,128)(2,1)}), bf16[32,2,2,32,1024]{4,3,2,1,0:T(8,128)(2,1)}, u32[]{:S(2)}, u32[]{:S(2)}) %all-to-all-start.1) | async-done | bytes 8388640 | tf_op jit(solution)/shard_map/all_to_all | solution.py:206
  385.5 8.5 %all-to-all-start.2 = ((bf16[32,2,32,1024]{3,2,1,0:T(8,128)(2,1)}), bf16[32,2,32,1024]{3,2,1,0:T(8,128)(2,1)}, u32[]{:S(2)}, u32[]{:S(2)}) async-start(bf16[32,2,32,1024]{3,2,1,0:T(8,128)(2,1)} %bitcast.126), calls=%async_computation.2 | async-start | bytes 8388608 | tf_op jit(solution)/shard_map/all_to_all | solution.py:206
  394.0 1.3 slice_bitcast_fusion.1
  396.5 2.6 concatenate.14
  399.1 1.6 copy-done.4
  400.7 50.7 %correlate.2 = bf16[16,2,2,32,1024]{4,3,2,1,0:T(8,128)(2,1)} custom-call(s32[2,2]{1,0:T(2,128)S(1)} %copy-done.1, bf16[1024,1024]{1,0:T(8,128)(2,1)S(1)} %copy-done.4, bf16[512,3072]{1,0:T(8,128)(2,1)S(1)} %copy-done.2, bf16[16,2,2,2,32,1024]{5,4,3,2,1,0:T(8,128)(2,1)} %bitcast.data), custom_call_target="tpu_custom_call" | custom-call | flops 30064771072 | bytes 12582912 | tf_op jit(solution)/shard_map/correlate/pallas_call | solution.py:97
  451.5 1.3 slice_bitcast_fusion
  454.1 2.2 maximum_bitcast_fusion
  457.0 1.5 copy-done.5
  458.5 1.9 fusion.25
  460.4 2.5 pad_maximum_fusion
  462.9 22.4 %all-to-all-done.2.refs_0_ = bf16[32,2,32,1024]{3,2,1,0:T(8,128)(2,1)} async-done(((bf16[32,2,32,1024]{3,2,1,0:T(8,128)(2,1)}), bf16[32,2,32,1024]{3,2,1,0:T(8,128)(2,1)}, u32[]{:S(2)}, u32[]{:S(2)}) %all-to-all-start.2) | async-done | bytes 4194336 | tf_op jit(solution)/shard_map/all_to_all | solution.py:206
  485.4 98.1 %all_to_all.25.refs_0_ = bf16[32,2,64,512]{3,2,1,0:T(8,128)(2,1)} all-to-all(bf16[32,2,64,512]{3,2,1,0:T(8,128)(2,1)} %pad_maximum_fusion), channel_id=1, replica_groups=mesh['energy'=16,'mom'=2] {'energy','mom'}, dimensions={0} | all-to-all | bytes 8388608 | tf_op jit(solution)/shard_map/all_to_all | solution.py:206
  583.5 6.0 all-to-all-start.4
  589.5 4.5 unpack.3.refs_1_
  594.1 1.6 slice-done
  596.4 2.1 gather_fusion
  598.6 3.4 copy.34
  605.3 2.3 pad_maximum_fusion.1
  607.6 5.4 copy.35
  613.0 4.0 reshape.89
  616.9 2.2 copy-done
  619.1 3.2 unpack.4.refs_1_
  622.3 13.6 %all-to-all-done.4.refs_0_ = bf16[32,2,32,512]{3,2,1,0:T(8,128)(2,1)} async-done(((bf16[32,2,32,512]{3,2,1,0:T(8,128)(2,1)}), bf16[32,2,32,512]{3,2,1,0:T(8,128)(2,1)}, u32[]{:S(2)}, u32[]{:S(2)}) %all-to-all-start.4) | async-done | bytes 2097184 | tf_op jit(solution)/shard_map/all_to_all | solution.py:206
  635.9 2.8 unpack.5
  (38 shorter events, 7.2 us)
Async XLA Ops:
  8.3 187.6 %all-to-all-start = ((bf16[32,2,2,32,1024]{4,3,2,1,0:T(8,128)(2,1)}), bf16[32,2,2,32,1024]{4,3,2,1,0:T(8,128)(2,1)}, u32[]{:S(2)}, u32[]{:S(2)}) async-start(bf16[32,2,2,32,1024]{4,3,2,1,0:T(8,128)(2,1)} %pack.3), calls=%async_computation | async-start | bytes 16777216 | tf_op jit(solution)/shard_map/all_to_all | solution.py:206
  22.2 182.1 %copy-start.1 = (s32[2,2]{1,0:T(2,128)S(1)}, s32[2,2]{1,0:T(2,128)}, u32[]{:S(2)}) copy-start(s32[2,2]{1,0:T(2,128)} %shift.3) | copy-start | bytes 52
  22.2 182.1 %copy-start.2 = (bf16[512,3072]{1,0:T(8,128)(2,1)S(1)}, bf16[512,3072]{1,0:T(8,128)(2,1)}, u32[]{:S(2)}) copy-start(bf16[512,3072]{1,0:T(8,128)(2,1)} %constant.22.clone.backward) | copy-start | bytes 9437188
  195.9 189.6 %all-to-all-start.1 = ((bf16[32,2,2,32,1024]{4,3,2,1,0:T(8,128)(2,1)}), bf16[32,2,2,32,1024]{4,3,2,1,0:T(8,128)(2,1)}, u32[]{:S(2)}, u32[]{:S(2)}) async-start(bf16[32,2,2,32,1024]{4,3,2,1,0:T(8,128)(2,1)} %pack.2), calls=%async_computation.1 | async-start | bytes 16777216 | tf_op jit(solution)/shard_map/all_to_all | solution.py:206
  204.3 1.6 copy-start.3
  385.5 99.8 %all-to-all-start.2 = ((bf16[32,2,32,1024]{3,2,1,0:T(8,128)(2,1)}), bf16[32,2,32,1024]{3,2,1,0:T(8,128)(2,1)}, u32[]{:S(2)}, u32[]{:S(2)}) async-start(bf16[32,2,32,1024]{3,2,1,0:T(8,128)(2,1)} %bitcast.126), calls=%async_computation.2 | async-start | bytes 8388608 | tf_op jit(solution)/shard_map/all_to_all | solution.py:206
  399.1 1.6 copy-start.4
  452.9 1.2 copy-start.6
  456.3 2.2 copy-start.5
  583.5 6.0 copy-start.8
  583.5 52.4 %all-to-all-start.4 = ((bf16[32,2,32,512]{3,2,1,0:T(8,128)(2,1)}), bf16[32,2,32,512]{3,2,1,0:T(8,128)(2,1)}, u32[]{:S(2)}, u32[]{:S(2)}) async-start(bf16[32,2,32,512]{3,2,1,0:T(8,128)(2,1)} %get-tuple-element.9), calls=%async_computation.4 | async-start | bytes 4194304 | tf_op jit(solution)/shard_map/all_to_all | solution.py:206
  594.1 1.6 slice-start
  602.0 0.9 copy-start.7
  616.9 2.2 copy-start

commit v5 on v4

--- a/solution.py
+++ b/solution.py
@@ -137,12 +137,21 @@
 
 def pack_kernel(start, lesser, greater, out, buffer, arrived, left):
     devices, _, _, _, width = out.shape
-    pairs = []
+    inward, outward = [], []
     for index in range(devices):
         columns = pl.ds(start + index * width, width)
         for side, array in enumerate((lesser, greater)):
-            pairs.append((array.at[0, :, :, columns], buffer.at[index, side], out.at[index, side]))
-    stage(pairs, arrived, left)
+            source, signal = array.at[0, :, :, columns], arrived.at[2 * index + side]
+            inward.append(pltpu.make_async_copy(source, buffer.at[index, side], signal))
+        outward.append(pltpu.make_async_copy(buffer.at[index], out.at[index], left.at[index]))
+    for copy in inward:
+        copy.start()
+    for index, copy in enumerate(outward):
+        inward[2 * index].wait()
+        inward[2 * index + 1].wait()
+        copy.start()
+    for copy in outward:
+        copy.wait()
 
 
 def pack(lesser, greater, start, width, devices):

time: 643 us -> 644 us (level)
  no operation moved by 1% of the time
where the time goes in v5:
time: 644 us; the launch traced here: 639 us
  waiting for transfers between devices  338 us (52%)
  Pallas kernels  128 us (20%)
  blocking collectives  98.1 us (15%)
  local copies, waits for them, and re-layouts  34.9 us (5%)
  starting transfers between devices  29 us (5%)
  other arithmetic  7.55 us (1%)
    all_to_all x4, waiting for transfers between devices, exchange(): return lax.all_to_all(array, AXES, split_axis=0, concat_axis=0, tiled=True)  338 us
    pallas_call x2, Pallas kernels, correlate(): pl.pallas_call(correlate_kernel, grid=(columns // width,), in_specs=[pl.B...  102 us
    all_to_all x1, blocking collectives, exchange(): return lax.all_to_all(array, AXES, split_axis=0, concat_axis=0, tiled=True)  98.1 us
    all_to_all x4, starting transfers between devices, exchange(): return lax.all_to_all(array, AXES, split_axis=0, concat_axis=0, tiled=True)  29 us
    pallas_call x2, Pallas kernels, pack(): pl.pallas_call(functools.partial(pack_kernel, start), in_specs=[pl.BlockS...  15.6 us
  transfers between devices with their start and end apart: 4, of which 4 were waited for; matrix products, arithmetic and copies ran while one was open for 6% of the time, Pallas kernels for 18%

profile of v5, /device:TPU:29, one launch (start us, length us, event | category | flops | bytes accessed | tf_op | source)
XLA Modules:
  0.0 639.0 jit_solution(4992294232749428144)
XLA Ops:
  0.6 7.8 %pack.3 = bf16[32,2,2,32,1024]{4,3,2,1,0:T(8,128)(2,1)} custom-call(bf16[1,2,32,65536]{3,2,1,0:T(8,128)(2,1)} %lesser.3, bf16[1,2,32,65536]{3,2,1,0:T(8,128)(2,1)} %greater.3), custom_call_target="tpu_custom_call" | custom-call | bytes 16777216 | tf_op jit(solution)/shard_map/pack/pallas_call | solution.py:162
  8.4 6.2 all-to-all-start
  14.6 7.8 %pack.2 = bf16[32,2,2,32,1024]{4,3,2,1,0:T(8,128)(2,1)} custom-call(bf16[1,2,32,65536]{3,2,1,0:T(8,128)(2,1)} %lesser.3, bf16[1,2,32,65536]{3,2,1,0:T(8,128)(2,1)} %greater.3), custom_call_target="tpu_custom_call" | custom-call | bytes 16777216 | tf_op jit(solution)/shard_map/pack/pallas_call | solution.py:162
  22.5 173.6 %all-to-all-done = bf16[32,2,2,32,1024]{4,3,2,1,0:T(8,128)(2,1)} async-done(((bf16[32,2,2,32,1024]{4,3,2,1,0:T(8,128)(2,1)}), bf16[32,2,2,32,1024]{4,3,2,1,0:T(8,128)(2,1)}, u32[]{:S(2)}, u32[]{:S(2)}) %all-to-all-start) | async-done | bytes 8388640 | tf_op jit(solution)/shard_map/all_to_all | solution.py:215
  196.1 8.3 %all-to-all-start.1 = ((bf16[32,2,2,32,1024]{4,3,2,1,0:T(8,128)(2,1)}), bf16[32,2,2,32,1024]{4,3,2,1,0:T(8,128)(2,1)}, u32[]{:S(2)}, u32[]{:S(2)}) async-start(bf16[32,2,2,32,1024]{4,3,2,1,0:T(8,128)(2,1)} %pack.2), calls=%async_computation.1 | async-start | bytes 16777216 | tf_op jit(solution)/shard_map/all_to_all | solution.py:215
  204.4 1.6 copy-done.3
  206.0 50.9 %correlate.3 = bf16[16,2,2,32,1024]{4,3,2,1,0:T(8,128)(2,1)} custom-call(s32[2,2]{1,0:T(2,128)S(1)} %copy-done.1, bf16[1024,1024]{1,0:T(8,128)(2,1)S(1)} %copy-done.3, bf16[512,3072]{1,0:T(8,128)(2,1)S(1)} %copy-done.2, bf16[16,2,2,2,32,1024]{5,4,3,2,1,0:T(8,128)(2,1)} %bitcast.2.data), custom_call_target="tpu_custom_call" | custom-call | flops 30064771072 | bytes 12582912 | tf_op jit(solution)/shard_map/correlate/pallas_call | solution.py:97
  256.9 128.8 %all-to-all-done.1 = bf16[32,2,2,32,1024]{4,3,2,1,0:T(8,128)(2,1)} async-done(((bf16[32,2,2,32,1024]{4,3,2,1,0:T(8,128)(2,1)}), bf16[32,2,2,32,1024]{4,3,2,1,0:T(8,128)(2,1)}, u32[]{:S(2)}, u32[]{:S(2)}) %all-to-all-start.1) | async-done | bytes 8388640 | tf_op jit(solution)/shard_map/all_to_all | solution.py:215
  385.7 8.5 %all-to-all-start.2 = ((bf16[32,2,32,1024]{3,2,1,0:T(8,128)(2,1)}), bf16[32,2,32,1024]{3,2,1,0:T(8,128)(2,1)}, u32[]{:S(2)}, u32[]{:S(2)}) async-start(bf16[32,2,32,1024]{3,2,1,0:T(8,128)(2,1)} %bitcast.126), calls=%async_computation.2 | async-start | bytes 8388608 | tf_op jit(solution)/shard_map/all_to_all | solution.py:215
  394.1 1.3 slice_bitcast_fusion.1
  396.7 2.6 concatenate.14
  399.3 1.6 copy-done.4
  400.9 50.8 %correlate.2 = bf16[16,2,2,32,1024]{4,3,2,1,0:T(8,128)(2,1)} custom-call(s32[2,2]{1,0:T(2,128)S(1)} %copy-done.1, bf16[1024,1024]{1,0:T(8,128)(2,1)S(1)} %copy-done.4, bf16[512,3072]{1,0:T(8,128)(2,1)S(1)} %copy-done.2, bf16[16,2,2,2,32,1024]{5,4,3,2,1,0:T(8,128)(2,1)} %bitcast.data), custom_call_target="tpu_custom_call" | custom-call | flops 30064771072 | bytes 12582912 | tf_op jit(solution)/shard_map/correlate/pallas_call | solution.py:97
  451.6 1.3 slice_bitcast_fusion
  454.3 2.2 maximum_bitcast_fusion
  457.1 1.5 copy-done.5
  458.7 1.9 fusion.25
  460.6 2.5 pad_maximum_fusion
  463.1 22.4 %all-to-all-done.2.refs_0_ = bf16[32,2,32,1024]{3,2,1,0:T(8,128)(2,1)} async-done(((bf16[32,2,32,1024]{3,2,1,0:T(8,128)(2,1)}), bf16[32,2,32,1024]{3,2,1,0:T(8,128)(2,1)}, u32[]{:S(2)}, u32[]{:S(2)}) %all-to-all-start.2) | async-done | bytes 4194336 | tf_op jit(solution)/shard_map/all_to_all | solution.py:215
  485.5 98.1 %all_to_all.25.refs_0_ = bf16[32,2,64,512]{3,2,1,0:T(8,128)(2,1)} all-to-all(bf16[32,2,64,512]{3,2,1,0:T(8,128)(2,1)} %pad_maximum_fusion), channel_id=1, replica_groups=mesh['energy'=16,'mom'=2] {'energy','mom'}, dimensions={0} | all-to-all | bytes 8388608 | tf_op jit(solution)/shard_map/all_to_all | solution.py:215
  583.6 6.0 all-to-all-start.4
  589.7 4.5 unpack.3.refs_1_
  594.2 1.6 slice-done
  596.6 2.1 gather_fusion
  598.7 3.4 copy.34
  605.5 2.3 pad_maximum_fusion.1
  607.7 5.4 copy.35
  613.1 4.0 reshape.89
  617.1 2.2 copy-done
  619.3 3.2 unpack.4.refs_1_
  622.5 13.6 %all-to-all-done.4.refs_0_ = bf16[32,2,32,512]{3,2,1,0:T(8,128)(2,1)} async-done(((bf16[32,2,32,512]{3,2,1,0:T(8,128)(2,1)}), bf16[32,2,32,512]{3,2,1,0:T(8,128)(2,1)}, u32[]{:S(2)}, u32[]{:S(2)}) %all-to-all-start.4) | async-done | bytes 2097184 | tf_op jit(solution)/shard_map/all_to_all | solution.py:215
  636.0 2.8 unpack.5
  (38 shorter events, 7.2 us)
Async XLA Ops:
  8.4 187.6 %all-to-all-start = ((bf16[32,2,2,32,1024]{4,3,2,1,0:T(8,128)(2,1)}), bf16[32,2,2,32,1024]{4,3,2,1,0:T(8,128)(2,1)}, u32[]{:S(2)}, u32[]{:S(2)}) async-start(bf16[32,2,2,32,1024]{4,3,2,1,0:T(8,128)(2,1)} %pack.3), calls=%async_computation | async-start | bytes 16777216 | tf_op jit(solution)/shard_map/all_to_all | solution.py:215
  22.4 182.0 %copy-start.1 = (s32[2,2]{1,0:T(2,128)S(1)}, s32[2,2]{1,0:T(2,128)}, u32[]{:S(2)}) copy-start(s32[2,2]{1,0:T(2,128)} %shift.3) | copy-start | bytes 52
  22.5 182.0 %copy-start.2 = (bf16[512,3072]{1,0:T(8,128)(2,1)S(1)}, bf16[512,3072]{1,0:T(8,128)(2,1)}, u32[]{:S(2)}) copy-start(bf16[512,3072]{1,0:T(8,128)(2,1)} %constant.22.clone.backward) | copy-start | bytes 9437188
  196.1 189.6 %all-to-all-start.1 = ((bf16[32,2,2,32,1024]{4,3,2,1,0:T(8,128)(2,1)}), bf16[32,2,2,32,1024]{4,3,2,1,0:T(8,128)(2,1)}, u32[]{:S(2)}, u32[]{:S(2)}) async-start(bf16[32,2,2,32,1024]{4,3,2,1,0:T(8,128)(2,1)} %pack.2), calls=%async_computation.1 | async-start | bytes 16777216 | tf_op jit(solution)/shard_map/all_to_all | solution.py:215
  204.4 1.6 copy-start.3
  385.7 99.8 %all-to-all-start.2 = ((bf16[32,2,32,1024]{3,2,1,0:T(8,128)(2,1)}), bf16[32,2,32,1024]{3,2,1,0:T(8,128)(2,1)}, u32[]{:S(2)}, u32[]{:S(2)}) async-start(bf16[32,2,32,1024]{3,2,1,0:T(8,128)(2,1)} %bitcast.126), calls=%async_computation.2 | async-start | bytes 8388608 | tf_op jit(solution)/shard_map/all_to_all | solution.py:215
  399.3 1.6 copy-start.4
  453.0 1.2 copy-start.6
  456.5 2.2 copy-start.5
  583.6 6.0 copy-start.8
  583.6 52.4 %all-to-all-start.4 = ((bf16[32,2,32,512]{3,2,1,0:T(8,128)(2,1)}), bf16[32,2,32,512]{3,2,1,0:T(8,128)(2,1)}, u32[]{:S(2)}, u32[]{:S(2)}) async-start(bf16[32,2,32,512]{3,2,1,0:T(8,128)(2,1)} %get-tuple-element.9), calls=%async_computation.4 | async-start | bytes 4194304 | tf_op jit(solution)/shard_map/all_to_all | solution.py:215
  594.2 1.6 slice-start
  602.2 0.9 copy-start.7
  617.1 2.2 copy-start
